TPU v7x, 128 devices: a whole 4x4x4 slice. The times are simulated.
128 devices in a mesh: pre: 16 (over y, z), head: 8 (over x, core).
Axes of the slice: x: 4, y: 4, z: 4, core: 2. Of those that a mesh axis runs over, the one named last changes fastest.
Arguments:
- query_latent: bfloat16 [640, 128, 576], P('pre', 'head'), may hold values from -12 to 12
- prefix_cache: bfloat16 [80, 512, 576], P('pre'), may hold values from -4 to 4
- block_slot: int32 [10, 8], replicated, may hold values from 0 to 79, as said below
- sample_prompt: int32 [640], replicated, may hold values from 0 to 9, as said below
- suffix_cache: bfloat16 [640, 384, 576], P('pre'), may hold values from -4 to 4
- suffix_length: int32 [640], P('pre'), may hold values from 1 to 384
- value_map: bfloat16 [128, 512, 128], P('head'), may hold values from -3 to 3
- out_weight: bfloat16 [16384, 7168], P('head', 'pre'), may hold values from -0.046875 to 0.046875
Outputs:
- mixed: bfloat16 [640, 7168], P('head', 'pre')
Inputs may be any that keep to these rules, and one draw needn't show every extreme that they name: `sample_prompt`: each of the 10 prompts is named by exactly 64 samples. `block_slot`: every slot of prefix_cache is named exactly once.
All inputs are finite; a program needn't handle non-finite values.
Results may differ from a plain program's by a relative error of at most 0.0055.
Values may be sent and summed in bfloat16 or wider, within the bound.
A program may use at most 192 MiB of HBM per device.

v0:
```python
import math

import jax
import jax.numpy as jnp
from jax import lax
from jax.sharding import PartitionSpec as P

GROUP = 64


score_scale = 1.0 / math.sqrt(192.0)
masked_score = -1e30


def attend(queries, key_rows, live_mask, latent_width):
    scores = (
        lax.dot_general(
            queries, key_rows, (((2,), (2,)), ((0,), (0,))), preferred_element_type=jnp.float32
        )
        * score_scale
    )
    scores = jnp.where(live_mask, scores, masked_score)
    largest = jnp.max(scores, axis=2)
    weights = jnp.exp(scores - largest[..., None]).astype(jnp.bfloat16)
    weights = lax.optimization_barrier(weights)
    weight_sum = jnp.sum(weights.astype(jnp.float32), axis=2)
    summed = lax.dot_general(
        weights,
        key_rows[:, :, :latent_width],
        (((2,), (1,)), ((0,), (0,))),
        preferred_element_type=jnp.float32,
    )
    return (summed / weight_sum[..., None], largest + jnp.log(weight_sum))


def merge_pair(first_out, first_lse, second_out, second_lse):
    largest = jnp.maximum(first_lse, second_lse)
    first_weight = jnp.exp(first_lse - largest)
    second_weight = jnp.exp(second_lse - largest)
    weight_sum = first_weight + second_weight
    merged = (
        first_weight[..., None] * first_out + second_weight[..., None] * second_out
    ) / weight_sum[..., None]
    return (merged, largest + jnp.log(weight_sum))


def merge_many(source_parts, source_lse, own_part, own_lse):
    largest = jnp.maximum(jnp.max(source_lse, axis=0), own_lse)
    source_weight = jnp.exp(source_lse - largest[None])
    own_weight = jnp.exp(own_lse - largest)
    weight_sum = jnp.sum(source_weight, axis=0) + own_weight
    combined = (
        jnp.sum(source_weight[..., None] * source_parts, axis=0) + own_weight[..., None] * own_part
    )
    return combined / weight_sum[..., None]


def project(latent, value_weight):
    return jnp.einsum("shc,hcv->shv", latent, value_weight, precision=lax.Precision.HIGHEST)


def per_device(
    query_latent,
    prefix_cache,
    block_slot,
    sample_prompt,
    suffix_cache,
    suffix_length,
    value_map,
    out_weight,
):
    local_samples, head_count, feature_width = query_latent.shape
    latent_width = value_map.shape[1]
    slot_count = prefix_cache.shape[0]
    owner_count = lax.axis_size("pre")
    owner_index = lax.axis_index("pre")
    sample_count = local_samples * owner_count
    value_weight = value_map.astype(jnp.float32)
    members = jnp.argsort(sample_prompt, stable=True).reshape(-1, GROUP)
    gathered = lax.all_gather(query_latent, "pre", axis=0, tiled=True)
    flat_slots = block_slot.reshape(-1)
    global_slot = owner_index * slot_count + jnp.arange(slot_count, dtype=jnp.int32)
    slot_match = (flat_slots[None, :] == global_slot[:, None]).astype(jnp.int32)
    prompt_ids = jnp.arange(flat_slots.shape[0], dtype=jnp.int32) // block_slot.shape[1]
    slot_prompt = jnp.sum(slot_match * prompt_ids[None, :], axis=1)
    dense_out = jnp.zeros((sample_count, head_count, latent_width), jnp.float32)
    dense_lse = jnp.full((sample_count, head_count), masked_score, jnp.float32)
    for slot_index in range(slot_count):
        member_rows = members[slot_prompt[slot_index]]
        queries = gathered[member_rows].reshape(1, GROUP * head_count, feature_width)
        block_out, block_lse = attend(queries, prefix_cache[slot_index][None], True, latent_width)
        block_out = block_out.reshape(GROUP, head_count, latent_width)
        block_lse = block_lse.reshape(GROUP, head_count)
        merged_out, merged_lse = merge_pair(
            dense_out[member_rows], dense_lse[member_rows], block_out, block_lse
        )
        dense_out = dense_out.at[member_rows].set(merged_out)
        dense_lse = dense_lse.at[member_rows].set(merged_lse)
    positions = jnp.arange(suffix_cache.shape[1], dtype=jnp.int32)
    live_mask = (positions[None, :] < suffix_length[:, None])[:, None, :]
    suffix_out, suffix_lse = attend(query_latent, suffix_cache, live_mask, latent_width)
    lse_blocks = dense_lse.reshape(owner_count, local_samples, head_count)
    source_parts, source_lse = (
        lax.all_to_all(
            dense_out.reshape(owner_count, local_samples, head_count, latent_width),
            "pre",
            split_axis=0,
            concat_axis=0,
            tiled=True,
        ),
        lax.all_to_all(lse_blocks, "pre", split_axis=0, concat_axis=0, tiled=True),
    )
    heads_out = project(merge_many(source_parts, source_lse, suffix_out, suffix_lse), value_weight)
    heads_out = heads_out.astype(jnp.bfloat16).reshape(local_samples, -1)
    head_terms = jnp.dot(
        lax.all_gather(heads_out, "pre", axis=0, tiled=True),
        out_weight,
        preferred_element_type=jnp.float32,
    )
    return lax.psum_scatter(head_terms, "head", scatter_dimension=0, tiled=True).astype(
        jnp.bfloat16
    )


def solution(mesh):
    return jax.shard_map(
        per_device,
        mesh=mesh,
        in_specs=(
            P("pre", "head", None),
            P("pre", None, None),
            P(),
            P(),
            P("pre", None, None),
            P("pre"),
            P("head", None, None),
            P("head", "pre"),
        ),
        out_specs=P("head", "pre"),
        check_vma=False,
    )
```

profile of v0, /device:TPU:1, one launch (start us, length us, event | category | flops | bytes accessed | tf_op | source)
XLA Modules:
  0.0 777.8 jit_solution(6719445488223659228)
XLA Ops:
  15.3 5.1 sort.17
  24.2 10.0 %broadcast_in_dim.21 = f32[640,16,512]{2,1,0:T(8,128)} broadcast(f32[]{:T(128)} %constant.44.clone.1), dimensions={} | broadcast | bytes 20971524 | tf_op jit(solution)/shard_map/broadcast_in_dim | solution.py:86
  34.2 9.2 %gather_fusion.10 = f32[64,16,512]{2,1,0:T(8,128)} fusion(f32[640,16,512]{2,1,0:T(8,128)} %broadcast_in_dim.21, s32[1024]{0:T(1024)S(1)} %pad_clamp_fusion.4), kind=kCustom, calls=%fused_computation.10 | custom fusion | bytes 4194560 | tf_op jit(solution)/shard_map/gather | solution.py:95
  43.4 62.6 %all-gather.3.cloned.1.call-done = bf16[640,16,576]{2,1,0:T(8,128)(2,1)} async-done(((bf16[40,16,576]{2,1,0:T(8,128)(2,1)}), bf16[640,16,576]{2,1,0:T(8,128)(2,1)}) %all-gather.3.cloned.1.call-update) | async-done | bytes 11796496 | tf_op jit(solution)/shard_map/all_gather | solution.py:80
  106.0 5.5 gather_fusion.1
  111.5 2.1 multiply_reduce_fusion.5
  114.1 3.2 convolution_divide_fusion.4
  117.3 5.5 gather_fusion.3
  122.9 2.1 multiply_reduce_fusion.4
  125.5 3.2 convolution_divide_fusion.3
  128.7 5.5 gather_fusion.5
  134.2 2.1 multiply_reduce_fusion.3
  136.8 3.2 convolution_divide_fusion.2
  140.0 5.5 gather_fusion.7
  145.5 2.1 multiply_reduce_fusion.2
  148.2 3.3 convolution_divide_fusion.1
  151.5 5.5 gather_fusion.9
  157.1 2.1 multiply_reduce_fusion.1
  159.7 3.2 convolution_divide_fusion
  164.5 0.9 scatter_custom_fusion.1
  166.1 0.9 scatter_custom_fusion.2
  167.8 0.9 scatter_custom_fusion.3
  169.4 0.9 scatter_custom_fusion.4
  171.2 5.0 all-to-all-start
  176.2 4.1 add_divide_fusion.4
  180.3 9.9 %scatter_fusion = f32[640,16,512]{2,1,0:T(8,128)} fusion(f32[640,16,512]{2,1,0:T(8,128)} %broadcast_in_dim.21, s32[64]{0:T(128)S(1)} %get-tuple-element.35, f32[64,16,512]{2,1,0:T(8,128)} %add_divide_fusion.4), kind=kCustom, calls=%fused_computation.20 | custom fusion | bytes 6291712 | tf_op jit(solution)/shard_map/scatter | solution.py:97
  190.2 9.0 %gather_fusion.11 = f32[64,16,512]{2,1,0:T(8,128)} fusion(f32[640,16,512]{2,1,0:T(8,128)} %scatter_fusion, s32[1024]{0:T(1024)S(1)} %get-tuple-element.56), kind=kCustom, calls=%fused_computation.11 | custom fusion | bytes 4194560 | tf_op jit(solution)/shard_map/gather | solution.py:95
  199.2 4.0 add_divide_fusion.3
  203.2 10.0 %scatter_fusion.1 = f32[640,16,512]{2,1,0:T(8,128)} fusion(f32[640,16,512]{2,1,0:T(8,128)} %scatter_fusion, s32[64]{0:T(128)S(1)} %get-tuple-element.34, f32[64,16,512]{2,1,0:T(8,128)} %add_divide_fusion.3), kind=kCustom, calls=%fused_computation.21 | custom fusion | bytes 6291712 | tf_op jit(solution)/shard_map/scatter | solution.py:97
  213.2 9.0 %gather_fusion.12 = f32[64,16,512]{2,1,0:T(8,128)} fusion(f32[640,16,512]{2,1,0:T(8,128)} %scatter_fusion.1, s32[1024]{0:T(1024)S(1)} %get-tuple-element.55), kind=kCustom, calls=%fused_computation.12 | custom fusion | bytes 4194560 | tf_op jit(solution)/shard_map/gather | solution.py:95
  222.2 4.0 add_divide_fusion.2
  226.2 9.9 %scatter_fusion.2 = f32[640,16,512]{2,1,0:T(8,128)} fusion(f32[640,16,512]{2,1,0:T(8,128)} %scatter_fusion.1, s32[64]{0:T(128)S(1)} %get-tuple-element.33, f32[64,16,512]{2,1,0:T(8,128)} %add_divide_fusion.2), kind=kCustom, calls=%fused_computation.22 | custom fusion | bytes 6291712 | tf_op jit(solution)/shard_map/scatter | solution.py:97
  236.1 9.0 %gather_fusion.13 = f32[64,16,512]{2,1,0:T(8,128)} fusion(f32[640,16,512]{2,1,0:T(8,128)} %scatter_fusion.2, s32[1024]{0:T(1024)S(1)} %get-tuple-element.54), kind=kCustom, calls=%fused_computation.13 | custom fusion | bytes 4194560 | tf_op jit(solution)/shard_map/gather | solution.py:95
  245.1 4.0 add_divide_fusion.1
  249.2 10.0 %scatter_fusion.3 = f32[640,16,512]{2,1,0:T(8,128)} fusion(f32[640,16,512]{2,1,0:T(8,128)} %scatter_fusion.2, s32[64]{0:T(128)S(1)} %get-tuple-element.32, f32[64,16,512]{2,1,0:T(8,128)} %add_divide_fusion.1), kind=kCustom, calls=%fused_computation.23 | custom fusion | bytes 6291712 | tf_op jit(solution)/shard_map/scatter | solution.py:97
  259.1 9.0 %gather_fusion.14 = f32[64,16,512]{2,1,0:T(8,128)} fusion(f32[640,16,512]{2,1,0:T(8,128)} %scatter_fusion.3, s32[1024]{0:T(1024)S(1)} %get-tuple-element.53), kind=kCustom, calls=%fused_computation.14 | custom fusion | bytes 4194560 | tf_op jit(solution)/shard_map/gather | solution.py:95
  268.1 4.0 add_divide_fusion
  272.2 9.9 %scatter_fusion.4 = f32[640,16,512]{2,1,0:T(8,128)} fusion(f32[640,16,512]{2,1,0:T(8,128)} %scatter_fusion.3, s32[64]{0:T(128)S(1)} %get-tuple-element.31, f32[64,16,512]{2,1,0:T(8,128)} %add_divide_fusion), kind=kCustom, calls=%fused_computation.24 | custom fusion | bytes 6291712 | tf_op jit(solution)/shard_map/scatter | solution.py:97
  282.1 7.0 all-to-all-start.1
  289.5 8.9 %fusion.83 = (f32[40,16]{1,0:T(8,128)S(1)}, f32[40,16,384]{2,1,0:T(8,128)S(1)}) fusion(bf16[40,16,576]{2,1,0:T(8,128)(2,1)} %param.8, bf16[40,384,576]{1,2,0:T(8,128)(2,1)} %param.12, pred[40,384]{1,0:T(8,128)(4,1)S(1)} %iota_compare_fusion), kind=kOutput, calls=%fused_computation.173 | convolution fusion | flops 283852160 | bytes 19432960 | tf_op jit(solution)/shard_map/dot_general | solution.py:17
  301.5 358.9 %all-to-all-done.1 = f32[16,40,16,512]{3,2,1,0:T(8,128)} async-done(((f32[16,40,16,512]{3,2,1,0:T(8,128)}), f32[16,40,16,512]{3,2,1,0:T(8,128)}, u32[]{:S(2)}, u32[]{:S(2)}) %all-to-all-start.1) | async-done | bytes 20971552 | tf_op jit(solution)/shard_map/all_to_all | solution.py:104
  660.4 8.2 %multiply_reduce_fusion = f32[40,16,512]{2,1,0:T(8,128)S(1)} fusion(f32[16,40,16,512]{3,2,1,0:T(8,128)} %all-to-all-done.1, f32[16,40,16]{2,1,0:T(8,128)S(1)} %copy.49), kind=kLoop, calls=%fused_computation.25 | loop fusion | flops 10158080 | bytes 22323200 | tf_op jit(solution)/shard_map/reduce_sum | solution.py:53
  668.7 10.8 %add_divide_fusion.5 = f32[40,16,512]{2,1,0:T(8,128)} fusion(f32[40,16,512]{2,1,0:T(8,128)S(1)} %multiply_reduce_fusion, bf16[40,16,384]{2,1,0:T(8,128)(2,1)S(1)} %copy-done.2, bf16[40,384,576]{1,2,0:T(8,128)(2,1)} %param.12, f32[40,16]{1,0:T(8,128)S(1)} %copy.52, f32[40,16]{1,0:T(8,128)S(1)} %convert_reduce_fusion.5, f32[40,16]{1,0:T(8,128)S(1)} %copy.50), kind=kOutput, calls=%fused_computation.57 | convolution fusion | flops 252968960 | bytes 18849280 | tf_op jit(solution)/shard_map/dot_general | solution.py:27
  679.4 3.0 fusion.8
  683.2 52.5 %all-gather.5.cloned.1.call-done = bf16[640,2048]{1,0:T(8,128)(2,1)} async-done(((bf16[40,2048]{1,0:T(8,128)(2,1)}), bf16[640,2048]{1,0:T(8,128)(2,1)}) %all-gather.5.cloned.1.call-update) | async-done | bytes 2621456 | tf_op jit(solution)/shard_map/all_gather | solution.py:116
  735.7 4.9 fusion.84
  740.7 29.0 %reduce-scatter.2.cloned.1.call-done = f32[80,448]{1,0:T(8,128)} async-done(((f32[640,448]{1,0:T(8,128)}), f32[80,448]{1,0:T(8,128)}) %reduce-scatter.2.cloned.1.call-update) | async-done | bytes 143376 | tf_op jit(solution)/shard_map/reduce_scatter | solution.py:120
  769.7 1.6 convert_element_type.81
  (77 shorter events, 14.6 us)
Async XLA Ops:
  6.5 672.9 %copy-start = (bf16[16,512,128]{2,1,0:T(8,128)(2,1)S(1)}, bf16[16,512,128]{2,1,0:T(8,128)(2,1)}, u32[]{:S(2)}) copy-start(bf16[16,512,128]{2,1,0:T(8,128)(2,1)} %param.14) | copy-start | bytes 6291460
  6.5 99.4 %all-gather.3.cloned.1.call-start = ((), (), s32[]{:S(2)}) async-start(), calls=%async_computation.3 | async-start | bytes 13926400 | tf_op jit(solution)/shard_map/all_gather | solution.py:80
  171.2 110.9 %all-to-all-start = ((f32[16,1,640]{2,1,0:T(1,128)}), f32[16,1,640]{2,1,0:T(1,128)S(1)}, u32[]{:S(2)}, u32[]{:S(2)}) async-start(f32[16,1,640]{2,1,0:T(1,128)} %reshape.888), calls=%async_computation | async-start | bytes 81920 | tf_op jit(solution)/shard_map/all_to_all | solution.py:111
  282.1 7.3 copy-start.3
  282.1 378.3 %all-to-all-start.1 = ((f32[16,40,16,512]{3,2,1,0:T(8,128)}), f32[16,40,16,512]{3,2,1,0:T(8,128)}, u32[]{:S(2)}, u32[]{:S(2)}) async-start(f32[16,40,16,512]{3,2,1,0:T(8,128)} %bitcast.143), calls=%async_computation.1 | async-start | bytes 41943040 | tf_op jit(solution)/shard_map/all_to_all | solution.py:104
  289.1 446.6 %all-gather.5.cloned.1.call-start = ((), (), s32[]{:S(2)}) async-start(), calls=%async_computation.4 | async-start | bytes 2785280 | tf_op jit(solution)/shard_map/all_gather | solution.py:116
  298.6 0.8 copy-start.1
  301.5 367.2 %copy-start.2 = (bf16[40,16,384]{2,1,0:T(8,128)(2,1)S(1)}, bf16[40,16,384]{2,1,0:T(8,128)(2,1)}, u32[]{:S(2)}) copy-start(bf16[40,16,384]{2,1,0:T(8,128)(2,1)} %copy-done.1) | copy-start | bytes 1474564
  683.1 86.6 %reduce-scatter.2.cloned.1.call-start = ((), (), s32[]{:S(2)}) async-start(), calls=%async_computation.5 | async-start | bytes 1474560 | tf_op jit(solution)/shard_map/reduce_scatter | solution.py:120
Sparse Core Ops, SparseCore 0:
  9.5 96.3 all-gather.2
  683.2 52.4 all-gather.4
  740.8 28.8 reduce-scatter.1
where the time goes:
time: 782 us; the launch traced here: 778 us
  waiting for transfers between devices  504 us (64%)
  local copies, waits for them, and re-layouts  141 us (18%)
  matrix products  54.2 us (7%)
  other arithmetic  43.8 us (6%)
  between operations  22.9 us (3%)
  starting transfers between devices  12.3 us (2%)
    all_to_all x1, waiting for transfers between devices, per_device(): lax.all_to_all(dense_out.reshape(owner_count, local_samples, head_count,...  359 us
    all_gather x1, waiting for transfers between devices, per_device(): gathered = lax.all_gather(query_latent, 'pre', axis=0, tiled=True)  62.6 us
    all_gather x1, waiting for transfers between devices, per_device(): lax.all_gather(heads_out, 'pre', axis=0, tiled=True)  52.5 us
    scatter x5, local copies, waits for them, and re-layouts, per_device(): dense_out = dense_out.at[member_rows].set(merged_out)  49.7 us
    gather x5, local copies, waits for them, and re-layouts, per_device(): dense_out[member_rows]  45.1 us
    reduce_scatter x1, waiting for transfers between devices, per_device(): lax.psum_scatter(head_terms, 'head', scatter_dimension=0, tiled=True)  29 us
    gather x5, local copies, waits for them, and re-layouts, per_device(): gathered[member_rows].reshape(1, GROUP * head_count, feature_width)  27.6 us
    dot_general x6, matrix products, attend(): lax.dot_general(weights, key_rows[:, :, :latent_width], (((2,), (1,)), ((...  26.9 us
  transfers between devices with their start and end apart: 5, of which 4 were waited for; matrix products, arithmetic and copies ran while one was open for 18% of the time, Pallas kernels for 0%

commit v1 on v0

v1 whole, which is shorter than its diff:
```python
import functools
import math

import jax
import jax.numpy as jnp
from jax import lax
from jax.experimental import pallas as pl
from jax.experimental.pallas import tpu as pltpu
from jax.sharding import PartitionSpec as P

GROUP = 64
PRE = 16
HEAD = 8
NS = 40
SP = 48
NH = 16
LAT = 512
VD = 128
SUF = 384
WIN = 80
NSLOT = 5
NPROMPT = 10
NBUF = 4
MASKED = -1e30
SCALE2 = math.log2(math.e) / math.sqrt(192.0)

BF = jnp.bfloat16
F32 = jnp.float32
MESH = pl.DeviceIdType.MESH


def nt(a, b):
    return lax.dot_general(a, b, (((1,), (1,)), ((), ())), preferred_element_type=F32)


def nn(a, b):
    return lax.dot_general(a, b, (((1,), (0,)), ((), ())), preferred_element_type=F32)


def onehot(mask):
    return jnp.where(mask, 1.0, 0.0).astype(BF)


def iota(shape, dim):
    return lax.broadcasted_iota(jnp.int32, shape, dim)


def kernel(
    q_hbm, k_hbm, suf_hbm, vm_hbm, w_hbm, rank_row, rank_col, slots, lens,
    out,
    q_in, k_in, vm, w_in, sufbuf,
    tmat, q_t, qr, sendl, sendr, krl, krr,
    skl, skr, sq, qw, kw, rw,
    lat_s, lt_s, o_s, l_s, osr, lsr, lacc_s,
    ol, op, lps, orr, lr, lacc,
    suf_o, suf_l, hbuf, pb, rs,
    ld_sem, suf_sem, a2a_s, a2a_r, x_s, x_r, c_s, c_r, g1_s, g1_r, g2_s, g2_r, e_s, e_r,
):
    p = lax.axis_index("pre")
    h = lax.axis_index("head")
    x, c = h // 2, lax.rem(h, 2)
    y, z = p // 4, lax.rem(p, 4)
    win, half = p // 2, lax.rem(p, 2)
    wj = lax.rem(win, 4)

    def remote(src, dst, ssem, rsem, pre, head):
        return pltpu.make_async_remote_copy(
            src_ref=src, dst_ref=dst, send_sem=ssem, recv_sem=rsem,
            device_id={"pre": pre, "head": head}, device_id_type=MESH,
        )

    def around(fn):
        def body(d, carry):
            fn(lax.rem(p + d, PRE))
            return carry
        lax.fori_loop(1, PRE, body, 0)

    def lane(i):
        return pl.ds(pl.multiple_of(i * 128, 128), 128)

    load_k = pltpu.make_async_copy(k_hbm, k_in, ld_sem.at[0])
    load_q = pltpu.make_async_copy(q_hbm, q_in, ld_sem.at[1])
    load_v = pltpu.make_async_copy(vm_hbm, vm, ld_sem.at[2])
    load_w = pltpu.make_async_copy(w_hbm, w_in, ld_sem.at[3])
    load_k.start()
    load_q.start()

    def suf_load(n, slot):
        return pltpu.make_async_copy(suf_hbm.at[n], sufbuf.at[slot], suf_sem.at[slot])

    barrier = pltpu.get_barrier_semaphore()

    def greet_pre(other):
        pl.semaphore_signal(barrier, inc=1, device_id={"pre": other, "head": h}, device_id_type=MESH)

    around(greet_pre)

    def greet_head(d, carry):
        pl.semaphore_signal(
            barrier, inc=1, device_id={"pre": p, "head": lax.rem(h + d, HEAD)}, device_id_type=MESH
        )
        return carry

    lax.fori_loop(1, HEAD, greet_head, 0)

    def build_t(i, carry):
        row = iota((SP, NS * NH), 0)
        col = iota((SP, NS * NH), 1)
        tmat[i] = onehot((lax.shift_right_logical(col, 4) == row) & ((col & 15) == i))
        return carry

    lax.fori_loop(0, NH, build_t, 0)
    lacc_s[...] = jnp.zeros_like(lacc_s)
    lacc[...] = jnp.zeros_like(lacc)
    pl.semaphore_wait(barrier, PRE - 1 + HEAD - 1)

    load_k.wait()

    def stage_k(i, carry):
        top = pl.multiple_of(i * 32, 32)
        mine = pl.multiple_of(i * 32 + c * 16, 16)
        for b in range(NSLOT):
            sendl[i, b] = k_in[b, pl.ds(mine, 16), lane(x)]
            sendr[i, b] = jnp.concatenate(
                [k_in[b, pl.ds(top, 16), LAT:], k_in[b, pl.ds(top + 16, 16), LAT:]], axis=-1
            )
        return carry

    lax.fori_loop(0, PRE, stage_k, 0)

    def s1l(other, src):
        return remote(sendl.at[other], krl.at[pl.ds(src * NSLOT, NSLOT)],
                      a2a_s.at[0, other], a2a_r.at[0, src], other, h)

    def s1r(other, src):
        return remote(sendr.at[other], krr.at[pl.ds(src * NSLOT, NSLOT)],
                      a2a_s.at[1, other], a2a_r.at[1, src], other, h)

    def start1(other):
        s1l(other, p).start()
        s1r(other, p).start()

    around(start1)
    krl[pl.ds(p * NSLOT, NSLOT)] = sendl[p]
    krr[pl.ds(p * NSLOT, NSLOT)] = sendr[p]

    load_q.wait()
    load_v.start()
    load_w.start()
    for n in range(NBUF):
        suf_load(n, n).start()
    q_flat = q_in[...].reshape(NS * NH, LAT + 64)
    for g in range(2):
        t_part = tmat[g * 8:(g + 1) * 8].reshape(8 * SP, NS * NH)
        q_t[g * 8:(g + 1) * 8] = nn(t_part, q_flat).astype(BF).reshape(8, SP, LAT + 64)

    def s1q(other, src):
        return remote(q_t.at[other], qr.at[src], a2a_s.at[2, other], a2a_r.at[2, src], other, h)

    around(lambda other: s1q(other, p).start())
    qr[p] = q_t[p]

    def suffix_one(n, carry):
        slot = lax.rem(n, NBUF)
        suf_load(n, slot).wait()
        qn = q_in[n]
        kn = sufbuf[slot]
        t = nt(qn, kn) * SCALE2
        t = jnp.where(iota((NH, SUF), 1) < lens[n], t, MASKED)
        m = jnp.max(t, axis=1, keepdims=True)
        w = jnp.exp2(t - m).astype(BF)
        total = jnp.sum(w.astype(F32), axis=1, keepdims=True)
        o = nn(w, kn[:, :LAT]) / total
        lat_s[pl.ds(pl.multiple_of(n * NH, NH), NH)] = o.astype(BF)
        lse = m + jnp.log2(total)
        lacc_s[...] = jnp.where(iota((NH, 128), 1) == n, lse, lacc_s[...])

        @pl.when(n + NBUF < NS)
        def _():
            suf_load(n + NBUF, slot).start()

        return carry

    lax.fori_loop(0, 8, suffix_one, 0)

    def wait1(other):
        s1l(other, other).wait_recv()
        s1r(other, other).wait_recv()

    around(wait1)

    def pick(prompt, carry):
        for b in range(8):
            slot = slots[prompt * 8 + b]
            skl[b // 4, prompt * 4 + b % 4] = krl[slot]
        for hf in range(2):
            skr[hf, prompt] = krr[slots[prompt * 8 + hf * 4 + x]]
        return carry

    lax.fori_loop(0, NPROMPT, pick, 0)

    def s2l(other, src):
        first = 5 * (other // 8) + lax.rem(other // 2, 4)
        return remote(skl.at[lax.rem(other, 2), pl.ds(first * 4, 8)], kw.at[c, :, src, :, lane(x)],
                      a2a_s.at[3, other], a2a_r.at[3, src], other, h)

    def s2r(other, src):
        first = 5 * (other // 8) + lax.rem(other // 2, 4)
        return remote(skr.at[lax.rem(other, 2), first + c], rw.at[c * 4 + x, src],
                      a2a_s.at[4, other], a2a_r.at[4, src], other, h)

    def start2(other):
        s2l(other, p).start()
        s2r(other, p).start()

    around(start2)
    own = 5 * (win // 4) + wj
    kw[c, :, p, :, lane(x)] = skl[half, pl.ds(own * 4, 8)]
    rw[c * 4 + x, p] = skr[half, own + c]

    around(lambda other: s1q(other, other).wait_recv())
    q_all = qr[...].reshape(PRE * SP, LAT + 64)
    for g in range(2):
        pick_rows = onehot(iota((320, PRE * SP), 0) + g * 320 == rank_row[...])
        sq[g * 320:(g + 1) * 320] = nn(pick_rows, q_all).astype(BF)

    def s2q(other, src):
        return remote(sq.at[pl.ds(pl.multiple_of((other // 2) * WIN, 16), WIN)], qw.at[src],
                      a2a_s.at[5, other], a2a_r.at[5, src], other, h)

    around(lambda other: s2q(other, p).start())
    qw[p] = sq[pl.ds(pl.multiple_of(win * WIN, 16), WIN)]

    lax.fori_loop(8, 14, suffix_one, 0)

    def wait2(other):
        s2l(other, other).wait_recv()
        s2r(other, other).wait_recv()

    around(wait2)

    def x_copies(d, src_x):
        to = lax.rem(x + d, 4) * 2 + c
        return (
            remote(kw.at[c, :, :, :, lane(src_x)], kw.at[c, :, :, :, lane(src_x)],
                   x_s.at[0, d - 1], x_r.at[0, d - 1], p, to),
            remote(rw.at[c * 4 + src_x], rw.at[c * 4 + src_x],
                   x_s.at[1, d - 1], x_r.at[1, d - 1], p, to),
        )

    def core_copies(d, src_x, cc):
        to = x * 2 + (1 - c)
        return (
            remote(kw.at[cc, :, :, :, lane(src_x)], kw.at[cc, :, :, :, lane(src_x)],
                   c_s.at[0, d], c_r.at[0, d], p, to),
            remote(rw.at[cc * 4 + src_x], rw.at[cc * 4 + src_x],
                   c_s.at[1, d], c_r.at[1, d], p, to),
        )

    for d in (1, 3, 2):
        for copy in x_copies(d, x):
            copy.start()
    for copy in core_copies(0, x, c):
        copy.start()

    lax.fori_loop(14, NS, suffix_one, 0)

    load_v.wait()
    for g in range(2):
        t_part = tmat[g * 8:(g + 1) * 8].reshape(8 * SP, NS * NH)
        lt_s[g * 8:(g + 1) * 8] = nn(t_part, lat_s[...]).astype(BF).reshape(8, SP, LAT)

    def project_s(i, carry):
        o_s[i] = nn(lt_s[i], vm[i]).astype(BF)
        return carry

    lax.fori_loop(0, NH, project_s, 0)
    l_s[...] = jnp.broadcast_to(lacc_s[...][:, None, :], (NH, 8, 128))

    def s4o(other, src):
        return remote(o_s.at[other], osr.at[src], a2a_s.at[6, other], a2a_r.at[6, src], other, h)

    def s4l(other, src):
        return remote(l_s.at[other], lsr.at[src], a2a_s.at[7, other], a2a_r.at[7, src], other, h)

    def start4(other):
        s4o(other, p).start()
        s4l(other, p).start()

    around(start4)
    osr[p] = o_s[p]
    lsr[p] = l_s[p]

    for d in (1, 3, 2):
        for copy in x_copies(d, lax.rem(x + 4 - d, 4)):
            copy.wait_recv()
        for copy in core_copies(d, lax.rem(x + 4 - d, 4), c):
            copy.start()

    around(lambda other: s2q(other, other).wait_recv())
    for d in (0, 1, 3, 2):
        for copy in core_copies(d, lax.rem(x + 4 - d, 4), 1 - c):
            copy.wait_recv()

    def chunk(t, carry):
        rows = pl.ds(pl.multiple_of(t * 16, 16), 16)
        ab = (t + wj) // 4
        ql = qw[:, rows, :LAT].reshape(256, LAT)
        qrope = qw[:, rows, LAT:].reshape(256, 64)
        none = jnp.zeros_like(qrope)
        q_side = (jnp.concatenate([qrope, none], axis=-1), jnp.concatenate([none, qrope], axis=-1))
        rope = rw[pl.ds(ab * 4, 4)].reshape(1024, 128)
        scores = []
        for cc in range(2):
            keys = kw[cc, pl.ds(ab * 4, 4)].reshape(1024, LAT)
            scores.append((nt(ql, keys) + nt(q_side[cc], rope)) * SCALE2)
        m = jnp.maximum(
            jnp.max(scores[0], axis=1, keepdims=True), jnp.max(scores[1], axis=1, keepdims=True)
        )
        total = jnp.zeros((256, 1), F32)
        acc = jnp.zeros((256, LAT), F32)
        for cc in range(2):
            w = jnp.exp2(scores[cc] - m).astype(BF)
            total = total + jnp.sum(w.astype(F32), axis=1, keepdims=True)
            acc = acc + nn(w, kw[cc, pl.ds(ab * 4, 4)].reshape(1024, LAT))
        ol[:, rows] = (acc / total).astype(BF).reshape(NH, 16, LAT)
        lse = (m + jnp.log2(total)).reshape(NH, 16, 1)
        here = iota((NH, 16, 128), 2) == iota((NH, 16, 128), 1) + t * 16
        lacc[...] += jnp.sum(jnp.where(here, lse, 0.0), axis=1)
        return carry

    lax.fori_loop(0, WIN // 16, chunk, 0)
    lps[...] = jnp.broadcast_to(lacc[...][:, None, :], (NH, 8, 128))

    def s5o(other, src):
        return remote(op.at[other], orr.at[src // 2, :, lane(lax.rem(src, 2))],
                      a2a_s.at[8, other], a2a_r.at[8, src], other, h)

    def s5l(other, src):
        return remote(lps.at[other], lr.at[src], a2a_s.at[9, other], a2a_r.at[9, src], other, h)

    def start5(other):
        op[other] = nn(ol[other], vm[other]).astype(BF)
        s5o(other, p).start()
        s5l(other, p).start()

    around(start5)
    orr[win, :, lane(half)] = nn(ol[p], vm[p]).astype(BF)
    lr[p] = lps[p]

    def wait4(other):
        s4o(other, other).wait_recv()
        s4l(other, other).wait_recv()

    around(wait4)

    def spread(src, carry):
        rows = pl.ds(pl.multiple_of(src * NS, 8), NS)
        suf_o[rows] = osr[src].astype(F32)[:NS]
        row = jnp.broadcast_to(lsr[src][0:1], (NS, 128))
        col = jnp.sum(jnp.where(iota((NS, 128), 0) == iota((NS, 128), 1), row, 0.0), axis=1, keepdims=True)
        suf_l[rows] = jnp.broadcast_to(col, (NS, 128))
        return carry

    lax.fori_loop(0, PRE, spread, 0)

    def wait5(other):
        s5o(other, other).wait_recv()
        s5l(other, other).wait_recv()

    around(wait5)

    def merge(g, carry):
        rows = pl.ds(pl.multiple_of(g * 320, 64), 320)
        rank = rank_col[rows]
        pick_rows = onehot(iota((320, PRE * NS), 1) == rank)
        parts = nn(pick_rows, orr[...].reshape(PRE * NS, 2 * VD))
        at = iota((320, 128), 1)
        la = jnp.zeros((320, 128), F32)
        lb = jnp.zeros((320, 128), F32)
        for w in range(8):
            hit = (at == rank - w * WIN) & (at < WIN)
            la = la + jnp.where(hit, lr[2 * w][0:1], 0.0)
            lb = lb + jnp.where(hit, lr[2 * w + 1][0:1], 0.0)
        la = jnp.sum(la, axis=1, keepdims=True)
        lb = jnp.sum(lb, axis=1, keepdims=True)
        ls = suf_l[rows]
        top = jnp.maximum(jnp.maximum(la, lb), ls)
        ea, eb, es = jnp.exp2(la - top), jnp.exp2(lb - top), jnp.exp2(ls - top)
        merged = (ea * parts[:, :VD] + eb * parts[:, VD:] + es * suf_o[rows]) / (ea + eb + es)
        hbuf[rows, lane(p)] = merged.astype(BF)
        return carry

    lax.fori_loop(0, 2, merge, 0)

    def g_copy(rows, piece, dy, dz, ssem, rsem):
        view = hbuf.at[pl.ds(rows * 320, 320), lane(piece)]
        return remote(view, view, ssem, rsem, lax.rem(y + dy, 4) * 4 + lax.rem(z + dz, 4), h)

    def piece_of(by, bz):
        return lax.rem(y + 4 - by, 4) * 4 + lax.rem(z + 4 - bz, 4)

    def first(rows, d, piece):
        dy, dz = (0, d) if rows == 0 else (d, 0)
        return g_copy(rows, piece, dy, dz, g1_s.at[rows, d - 1], g1_r.at[rows, d - 1])

    def second(rows, k, d, piece):
        dy, dz = (d, 0) if rows == 0 else (0, d)
        return g_copy(rows, piece, dy, dz, g2_s.at[rows, k * 3 + d - 1], g2_r.at[rows, k * 3 + d - 1])

    for d in (1, 3, 2):
        for rows in range(2):
            first(rows, d, p).start()
    for d in (1, 3, 2):
        for rows in range(2):
            second(rows, 0, d, p).start()
    for k in (1, 3, 2):
        for rows in range(2):
            got = piece_of(0, k) if rows == 0 else piece_of(k, 0)
            first(rows, k, got).wait_recv()
            for d in (1, 3, 2):
                second(rows, k, d, got).start()
    for k in (0, 1, 3, 2):
        for d in (1, 3, 2):
            for rows in range(2):
                got = piece_of(d, k) if rows == 0 else piece_of(k, d)
                second(rows, k, d, got).wait_recv()

    load_w.wait()

    def out_rows(g, carry):
        rows = pl.ds(pl.multiple_of(g * 320, 64), 320)
        pb[pl.ds(g * 4, 4)] = nn(hbuf[rows], w_in[...]).astype(BF).reshape(4, WIN, 448)
        return carry

    lax.fori_loop(0, 2, out_rows, 0)

    def s6(other, src):
        return remote(pb.at[other], rs.at[src], e_s.at[other], e_r.at[src], p, other)

    def heads(fn):
        def body(d, carry):
            fn(lax.rem(h + d, HEAD))
            return carry
        lax.fori_loop(1, HEAD, body, 0)

    heads(lambda other: s6(other, h).start())
    rs[h] = pb[h]
    heads(lambda other: s6(other, other).wait_recv())
    total = rs[0].astype(F32)
    for k in range(1, HEAD):
        total = total + rs[k].astype(F32)
    out[...] = total.astype(BF)

    def sent(other):
        for copy in (s1l, s1r, s1q, s2l, s2r, s2q, s4o, s4l, s5o, s5l):
            copy(other, p).wait_send()

    around(sent)
    for d in (1, 2, 3):
        for copy in x_copies(d, x):
            copy.wait_send()
    for d in range(4):
        for copy in core_copies(d, lax.rem(x + 4 - d, 4), c):
            copy.wait_send()
    for rows in range(2):
        for d in (1, 2, 3):
            first(rows, d, p).wait_send()
        for k in range(4):
            for d in (1, 2, 3):
                second(rows, k, d, p).wait_send()
    heads(lambda other: s6(other, h).wait_send())


def per_device(
    query_latent, prefix_cache, block_slot, sample_prompt, suffix_cache, suffix_length, value_map, out_weight
):
    sp = sample_prompt
    n = jnp.arange(sp.shape[0], dtype=jnp.int32)
    earlier = (sp[None, :] == sp[:, None]) & (n[None, :] < n[:, None])
    rank = sp * GROUP + jnp.sum(earlier.astype(jnp.int32), axis=1)
    rank_row = jnp.pad(rank.reshape(PRE, NS), ((0, 0), (0, SP - NS)), constant_values=-1).reshape(1, PRE * SP)
    rank_col = rank.reshape(-1, 1)
    vmem = pl.BlockSpec(memory_space=pltpu.VMEM)
    smem = pl.BlockSpec(memory_space=pltpu.SMEM)
    hbm = pl.BlockSpec(memory_space=pl.ANY)
    V = pltpu.VMEM
    dma = pltpu.SemaphoreType.DMA
    width = LAT + 64
    scratch = [
        V((NS, NH, width), BF), V((NSLOT, 512, width), BF), V((NH, LAT, VD), BF), V((NH * VD, 448), BF),
        V((NBUF, SUF, width), BF),
        V((NH, SP, NS * NH), BF), V((NH, SP, width), BF), V((PRE, SP, width), BF),
        V((PRE, NSLOT, 16, 128), BF), V((PRE, NSLOT, 16, 128), BF),
        V((PRE * NSLOT, 16, 128), BF), V((PRE * NSLOT, 16, 128), BF),
        V((2, NPROMPT * 4, 16, 128), BF), V((2, NPROMPT, 16, 128), BF),
        V((PRE * NS, width), BF), V((NH, WIN, width), BF),
        V((2, 8, PRE, 16, LAT), BF), V((8, PRE, 16, 128), BF),
        V((NS * NH, LAT), BF), V((NH, SP, LAT), BF), V((NH, SP, VD), BF), V((NH, 8, 128), F32),
        V((PRE, SP, VD), BF), V((PRE, 8, 128), F32), V((NH, 128), F32),
        V((NH, WIN, LAT), BF), V((NH, WIN, VD), BF), V((NH, 8, 128), F32),
        V((8, WIN, 2 * VD), BF), V((PRE, 8, 128), F32), V((NH, 128), F32),
        V((PRE * NS, VD), F32), V((PRE * NS, 128), F32), V((PRE * NS, NH * VD), BF),
        V((HEAD, WIN, 448), BF), V((HEAD, WIN, 448), BF),
        dma((4,)), dma((NBUF,)), dma((10, PRE)), dma((10, PRE)),
        dma((2, 3)), dma((2, 3)), dma((2, 4)), dma((2, 4)),
        dma((2, 3)), dma((2, 3)), dma((2, 12)), dma((2, 12)), dma((HEAD,)), dma((HEAD,)),
    ]
    return pl.pallas_call(
        kernel,
        out_shape=jax.ShapeDtypeStruct((WIN, 448), BF),
        in_specs=[hbm, hbm, hbm, hbm, hbm, vmem, vmem, smem, smem],
        out_specs=vmem,
        scratch_shapes=scratch,
        compiler_params=pltpu.CompilerParams(
            collective_id=0, has_side_effects=True, vmem_limit_bytes=58 * 1024 * 1024
        ),
        cost_estimate=pl.CostEstimate(flops=10_000_000_000, bytes_accessed=30_000_000, transcendentals=3_000_000),
    )(
        query_latent, prefix_cache, suffix_cache, value_map, out_weight,
        rank_row, rank_col, block_slot.reshape(-1), suffix_length,
    )


def solution(mesh):
    return jax.shard_map(
        per_device,
        mesh=mesh,
        in_specs=(
            P("pre", "head", None),
            P("pre", None, None),
            P(),
            P(),
            P("pre", None, None),
            P("pre"),
            P("head", None, None),
            P("head", "pre"),
        ),
        out_specs=P("head", "pre"),
        check_vma=False,
    )
```

time: 782 us -> 183 us (0.23)
  waiting for transfers between devices: 504 us -> 0 us
  Pallas kernels: 0 us -> 144 us
  local copies, waits for them, and re-layouts: 141 us -> 36.2 us
  matrix products: 54.2 us -> 0 us
  other arithmetic: 43.8 us -> 1.75 us
  between operations: 22.9 us -> 0.03 us
  starting transfers between devices: 12.3 us -> 0 us
    all_to_all x2 -> x0, waiting for transfers between devices: 359 us -> none  [the longest x1 359 us: per_device(): lax.all_to_all(dense_out.reshape(owner_count, local_samples, head_count,...]
    pallas_call x0 -> x1, Pallas kernels: none -> 144 us  [per_device(): pl.pallas_call(kernel, out_shape=jax.ShapeDtypeStruct((WIN, 448), BF), in...]
    all_gather x2 -> x0, waiting for transfers between devices: 115 us -> none  [the longest x1 62.6 us: per_device(): gathered = lax.all_gather(query_latent, 'pre', axis=0, tiled=True)]
    gather x15 -> x0, local copies, waits for them, and re-layouts: 75.7 us -> none  [the longest x5 45.1 us: per_device(): dense_out[member_rows]]
    dot_general x14 -> x0, matrix products: 54.2 us -> none  [the longest x6 26.9 us: attend(): lax.dot_general(weights, key_rows[:, :, :latent_width], (((2,), (1,)), ((...]
    scatter x5 -> x0, local copies, waits for them, and re-layouts: 49.7 us -> none  [per_device(): dense_out = dense_out.at[member_rows].set(merged_out)]
    unnamed x11 -> x7, local copies, waits for them, and re-layouts: 2.49 us -> 33.9 us
    reduce_scatter x1 -> x0, waiting for transfers between devices: 29 us -> none  [per_device(): lax.psum_scatter(head_terms, 'head', scatter_dimension=0, tiled=True)]
  transfers between devices with their start and end apart: 5 -> 0, of which waited for: 4 -> 0; matrix products, arithmetic and copies ran while one was open for 18% -> 0% of each run, Pallas kernels for 0% -> 0%
where the time goes in v1:
time: 183 us; the launch traced here: 182 us
  Pallas kernels  144 us (79%)
  local copies, waits for them, and re-layouts  36.2 us (20%)
    pallas_call x1, Pallas kernels, per_device(): pl.pallas_call(kernel, out_shape=jax.ShapeDtypeStruct((WIN, 448), BF), in...  144 us
    unnamed x7, local copies, waits for them, and re-layouts  33.9 us

profile of v1, /device:TPU:1, one launch (start us, length us, event | category | flops | bytes accessed | tf_op | source)
XLA Modules:
  0.0 182.3 jit_solution(5155322008843977183)
XLA Ops:
  0.0 1.1 convert_reduce_fusion
  1.1 0.7 multiply_add_fusion
  1.8 0.1 reshape.14
  1.9 0.7 reshape.15.rank_row
  2.5 0.8 copy.18
  3.3 0.6 reshape.17.slots
  3.9 0.0 copy-start
  3.9 0.9 reshape.18.rank_col
  4.8 3.9 %copy.21.w_hbm = bf16[2048,448]{1,0:T(8,128)(2,1)} copy(bf16[2048,448]{0,1:T(8,128)(2,1)} %param.15) | data formatting | bytes 3670016 | tf_op args[7]
  8.7 0.0 copy-done
  8.7 3.2 %copy.19.k_hbm = bf16[5,512,576]{2,1,0:T(8,128)(2,1)} copy(bf16[5,512,576]{1,2,0:T(8,128)(2,1)S(1)} %copy-done) | data formatting | bytes 5898240 | tf_op args[1]
  11.9 24.5 %copy.20.suf_hbm = bf16[40,384,576]{2,1,0:T(8,128)(2,1)} copy(bf16[40,384,576]{1,2,0:T(8,128)(2,1)} %param.12) | data formatting | bytes 35389440 | tf_op args[4]
  36.4 144.3 %shard_map.82 = bf16[80,448]{1,0:T(8,128)(2,1)} custom-call(bf16[40,16,576]{2,1,0:T(8,128)(2,1)} %q_hbm.1, bf16[5,512,576]{2,1,0:T(8,128)(2,1)} %copy.19.k_hbm, bf16[40,384,576]{2,1,0:T(8,128)(2,1)} %copy.20.suf_hbm, bf16[16,512,128]{2,1,0:T(8,128)(2,1)} %vm_hbm.1, bf16[2048,448]{1,0:T(8,128)(2,1)} %copy.21.w_hbm, s32[1,768]{1,0:T(1,128)} %reshape.15.rank_row, ...), custom_call_target="tpu_custom_call" | custom-call | flops 10000000000 | bytes 30000000 | tf_op jit(solution)/shard_map/pallas_call | solution.py:509
  180.7 1.5 copy.24
  (1 shorter events, 0.0 us)
Async XLA Ops:
  3.9 4.8 %copy-start = (bf16[5,512,576]{1,2,0:T(8,128)(2,1)S(1)}, bf16[5,512,576]{1,2,0:T(8,128)(2,1)}, u32[]{:S(2)}) copy-start(bf16[5,512,576]{1,2,0:T(8,128)(2,1)} %param.9) | copy-start | bytes 8847364

commit v2 on v1

--- a/solution.py
+++ b/solution.py
@@ -46,11 +46,11 @@
 
 
 def kernel(
-    q_hbm, k_hbm, suf_hbm, vm_hbm, w_hbm, rank_row, rank_col, slots, lens,
+    q_hbm, k_hbm, suf_hbm, vm_hbm, w_hbm, prompt_row, slots, lens,
     out,
-    q_in, k_in, vm, w_in, sufbuf,
-    tmat, q_t, qr, sendl, sendr, krl, krr,
-    skl, skr, sq, qw, kw, rw,
+    q_in, vm, w_in, sufbuf,
+    tmat, q_t, qr, krl, krr,
+    skl, skr, sq, qw, kw, rank_row, rank_col,
     lat_s, lt_s, o_s, l_s, osr, lsr, lacc_s,
     ol, op, lps, orr, lr, lacc,
     suf_o, suf_l, hbuf, pb, rs,
@@ -78,11 +78,9 @@
     def lane(i):
         return pl.ds(pl.multiple_of(i * 128, 128), 128)
 
-    load_k = pltpu.make_async_copy(k_hbm, k_in, ld_sem.at[0])
-    load_q = pltpu.make_async_copy(q_hbm, q_in, ld_sem.at[1])
+    load_q = pltpu.make_async_copy(q_hbm, q_in, ld_sem.at[4])
     load_v = pltpu.make_async_copy(vm_hbm, vm, ld_sem.at[2])
     load_w = pltpu.make_async_copy(w_hbm, w_in, ld_sem.at[3])
-    load_k.start()
     load_q.start()
 
     def suf_load(n, slot):
@@ -110,30 +108,37 @@
         return carry
 
     lax.fori_loop(0, NH, build_t, 0)
+
+    names = jnp.broadcast_to(prompt_row[...], (SP, PRE * SP))
+    at = iota((SP, PRE * SP), 1)
+    rank_row[...] = prompt_row[...] * GROUP
+
+    def build_rank(i, carry):
+        ids = iota((SP, PRE * SP), 0) + i * SP
+        name = jnp.sum(jnp.where(at == ids, names, 0), axis=1, keepdims=True)
+        same = names == name
+        before = jnp.sum(jnp.where(same & (at < ids), 1, 0), axis=1, keepdims=True)
+        rank_col[pl.ds(pl.multiple_of(i * NS, 8), NS)] = (name * GROUP + before)[:NS]
+        rank_row[...] += jnp.sum(jnp.where(same & (ids < at), 1, 0), axis=0, keepdims=True)
+        return carry
+
+    lax.fori_loop(0, PRE, build_rank, 0)
     lacc_s[...] = jnp.zeros_like(lacc_s)
     lacc[...] = jnp.zeros_like(lacc)
     pl.semaphore_wait(barrier, PRE - 1 + HEAD - 1)
 
-    load_k.wait()
-
-    def stage_k(i, carry):
-        top = pl.multiple_of(i * 32, 32)
-        mine = pl.multiple_of(i * 32 + c * 16, 16)
-        for b in range(NSLOT):
-            sendl[i, b] = k_in[b, pl.ds(mine, 16), lane(x)]
-            sendr[i, b] = jnp.concatenate(
-                [k_in[b, pl.ds(top, 16), LAT:], k_in[b, pl.ds(top + 16, 16), LAT:]], axis=-1
-            )
-        return carry
-
-    lax.fori_loop(0, PRE, stage_k, 0)
+    def tiles(i):
+        return (
+            k_hbm.at[:, pl.ds(pl.multiple_of(c * 256 + i * 16, 16), 16), lane(x)],
+            k_hbm.at[:, pl.ds(pl.multiple_of(LAT + lax.rem(i, 4) * 16, 16), 16), lane(x)],
+        )
 
     def s1l(other, src):
-        return remote(sendl.at[other], krl.at[pl.ds(src * NSLOT, NSLOT)],
+        return remote(tiles(other)[0], krl.at[pl.ds(src * NSLOT, NSLOT)],
                       a2a_s.at[0, other], a2a_r.at[0, src], other, h)
 
     def s1r(other, src):
-        return remote(sendr.at[other], krr.at[pl.ds(src * NSLOT, NSLOT)],
+        return remote(tiles(other)[1], krr.at[pl.ds(src * NSLOT, NSLOT)],
                       a2a_s.at[1, other], a2a_r.at[1, src], other, h)
 
     def start1(other):
@@ -141,8 +146,10 @@
         s1r(other, p).start()
 
     around(start1)
-    krl[pl.ds(p * NSLOT, NSLOT)] = sendl[p]
-    krr[pl.ds(p * NSLOT, NSLOT)] = sendr[p]
+    own_l = pltpu.make_async_copy(tiles(p)[0], krl.at[pl.ds(p * NSLOT, NSLOT)], ld_sem.at[0])
+    own_r = pltpu.make_async_copy(tiles(p)[1], krr.at[pl.ds(p * NSLOT, NSLOT)], ld_sem.at[1])
+    own_l.start()
+    own_r.start()
 
     load_q.wait()
     load_v.start()
@@ -165,12 +172,12 @@
         suf_load(n, slot).wait()
         qn = q_in[n]
         kn = sufbuf[slot]
-        t = nt(qn, kn) * SCALE2
+        t = nn(qn, kn) * SCALE2
         t = jnp.where(iota((NH, SUF), 1) < lens[n], t, MASKED)
         m = jnp.max(t, axis=1, keepdims=True)
         w = jnp.exp2(t - m).astype(BF)
         total = jnp.sum(w.astype(F32), axis=1, keepdims=True)
-        o = nn(w, kn[:, :LAT]) / total
+        o = nt(w, kn[:LAT]) / total
         lat_s[pl.ds(pl.multiple_of(n * NH, NH), NH)] = o.astype(BF)
         lse = m + jnp.log2(total)
         lacc_s[...] = jnp.where(iota((NH, 128), 1) == n, lse, lacc_s[...])
@@ -188,25 +195,29 @@
         s1r(other, other).wait_recv()
 
     around(wait1)
+    own_l.wait()
+    own_r.wait()
 
     def pick(prompt, carry):
         for b in range(8):
-            slot = slots[prompt * 8 + b]
+            slot = slots[b, prompt]
             skl[b // 4, prompt * 4 + b % 4] = krl[slot]
         for hf in range(2):
-            skr[hf, prompt] = krr[slots[prompt * 8 + hf * 4 + x]]
+            skr[hf, prompt] = krr[slots[hf * 4 + p // 4, prompt]]
         return carry
 
     lax.fori_loop(0, NPROMPT, pick, 0)
 
     def s2l(other, src):
         first = 5 * (other // 8) + lax.rem(other // 2, 4)
-        return remote(skl.at[lax.rem(other, 2), pl.ds(first * 4, 8)], kw.at[c, :, src, :, lane(x)],
+        rows = pl.ds(pl.multiple_of(c * 256 + src * 16, 16), 16)
+        return remote(skl.at[lax.rem(other, 2), pl.ds(first * 4, 8)], kw.at[:, rows, lane(x)],
                       a2a_s.at[3, other], a2a_r.at[3, src], other, h)
 
     def s2r(other, src):
         first = 5 * (other // 8) + lax.rem(other // 2, 4)
-        return remote(skr.at[lax.rem(other, 2), first + c], rw.at[c * 4 + x, src],
+        rows = pl.ds(pl.multiple_of(LAT + lax.rem(src, 4) * 16, 16), 16)
+        return remote(skr.at[lax.rem(other, 2), first + c], kw.at[c * 4 + src // 4, rows, lane(x)],
                       a2a_s.at[4, other], a2a_r.at[4, src], other, h)
 
     def start2(other):
@@ -215,8 +226,8 @@
 
     around(start2)
     own = 5 * (win // 4) + wj
-    kw[c, :, p, :, lane(x)] = skl[half, pl.ds(own * 4, 8)]
-    rw[c * 4 + x, p] = skr[half, own + c]
+    kw[:, pl.ds(pl.multiple_of(c * 256 + p * 16, 16), 16), lane(x)] = skl[half, pl.ds(own * 4, 8)]
+    kw[c * 4 + p // 4, pl.ds(pl.multiple_of(LAT + lax.rem(p, 4) * 16, 16), 16), lane(x)] = skr[half, own + c]
 
     around(lambda other: s1q(other, other).wait_recv())
     q_all = qr[...].reshape(PRE * SP, LAT + 64)
@@ -239,23 +250,23 @@
 
     around(wait2)
 
+    def part(cc, src_x):
+        rows = pl.ds(pl.multiple_of(cc * 256, 256), 256)
+        return kw.at[:, rows, lane(src_x)], kw.at[pl.ds(cc * 4, 4), LAT:, lane(src_x)]
+
     def x_copies(d, src_x):
         to = lax.rem(x + d, 4) * 2 + c
-        return (
-            remote(kw.at[c, :, :, :, lane(src_x)], kw.at[c, :, :, :, lane(src_x)],
-                   x_s.at[0, d - 1], x_r.at[0, d - 1], p, to),
-            remote(rw.at[c * 4 + src_x], rw.at[c * 4 + src_x],
-                   x_s.at[1, d - 1], x_r.at[1, d - 1], p, to),
-        )
+        return [
+            remote(view, view, x_s.at[k, d - 1], x_r.at[k, d - 1], p, to)
+            for k, view in enumerate(part(c, src_x))
+        ]
 
     def core_copies(d, src_x, cc):
         to = x * 2 + (1 - c)
-        return (
-            remote(kw.at[cc, :, :, :, lane(src_x)], kw.at[cc, :, :, :, lane(src_x)],
-                   c_s.at[0, d], c_r.at[0, d], p, to),
-            remote(rw.at[cc * 4 + src_x], rw.at[cc * 4 + src_x],
-                   c_s.at[1, d], c_r.at[1, d], p, to),
-        )
+        return [
+            remote(view, view, c_s.at[k, d], c_r.at[k, d], p, to)
+            for k, view in enumerate(part(cc, src_x))
+        ]
 
     for d in (1, 3, 2):
         for copy in x_copies(d, x):
@@ -305,24 +316,15 @@
     def chunk(t, carry):
         rows = pl.ds(pl.multiple_of(t * 16, 16), 16)
         ab = (t + wj) // 4
-        ql = qw[:, rows, :LAT].reshape(256, LAT)
-        qrope = qw[:, rows, LAT:].reshape(256, 64)
-        none = jnp.zeros_like(qrope)
-        q_side = (jnp.concatenate([qrope, none], axis=-1), jnp.concatenate([none, qrope], axis=-1))
-        rope = rw[pl.ds(ab * 4, 4)].reshape(1024, 128)
-        scores = []
-        for cc in range(2):
-            keys = kw[cc, pl.ds(ab * 4, 4)].reshape(1024, LAT)
-            scores.append((nt(ql, keys) + nt(q_side[cc], rope)) * SCALE2)
-        m = jnp.maximum(
-            jnp.max(scores[0], axis=1, keepdims=True), jnp.max(scores[1], axis=1, keepdims=True)
-        )
+        qc = qw[:, rows].reshape(256, LAT + 64)
+        scores = [nn(qc, kw[ab * 4 + b]) * SCALE2 for b in range(4)]
+        m = functools.reduce(jnp.maximum, [jnp.max(t, axis=1, keepdims=True) for t in scores])
         total = jnp.zeros((256, 1), F32)
         acc = jnp.zeros((256, LAT), F32)
-        for cc in range(2):
-            w = jnp.exp2(scores[cc] - m).astype(BF)
+        for b in range(4):
+            w = jnp.exp2(scores[b] - m).astype(BF)
             total = total + jnp.sum(w.astype(F32), axis=1, keepdims=True)
-            acc = acc + nn(w, kw[cc, pl.ds(ab * 4, 4)].reshape(1024, LAT))
+            acc = acc + nt(w, kw[ab * 4 + b, :LAT])
         ol[:, rows] = (acc / total).astype(BF).reshape(NH, 16, LAT)
         lse = (m + jnp.log2(total)).reshape(NH, 16, 1)
         here = iota((NH, 16, 128), 2) == iota((NH, 16, 128), 1) + t * 16
@@ -430,7 +432,7 @@
 
     def out_rows(g, carry):
         rows = pl.ds(pl.multiple_of(g * 320, 64), 320)
-        pb[pl.ds(g * 4, 4)] = nn(hbuf[rows], w_in[...]).astype(BF).reshape(4, WIN, 448)
+        pb[pl.ds(g * 4, 4)] = nt(hbuf[rows], w_in[...]).astype(BF).reshape(4, WIN, 448)
         return carry
 
     lax.fori_loop(0, 2, out_rows, 0)
@@ -475,12 +477,9 @@
 def per_device(
     query_latent, prefix_cache, block_slot, sample_prompt, suffix_cache, suffix_length, value_map, out_weight
 ):
-    sp = sample_prompt
-    n = jnp.arange(sp.shape[0], dtype=jnp.int32)
-    earlier = (sp[None, :] == sp[:, None]) & (n[None, :] < n[:, None])
-    rank = sp * GROUP + jnp.sum(earlier.astype(jnp.int32), axis=1)
-    rank_row = jnp.pad(rank.reshape(PRE, NS), ((0, 0), (0, SP - NS)), constant_values=-1).reshape(1, PRE * SP)
-    rank_col = rank.reshape(-1, 1)
+    prompt_row = jnp.pad(
+        sample_prompt.reshape(PRE, NS), ((0, 0), (0, SP - NS)), constant_values=-4
+    ).reshape(1, PRE * SP)
     vmem = pl.BlockSpec(memory_space=pltpu.VMEM)
     smem = pl.BlockSpec(memory_space=pltpu.SMEM)
     hbm = pl.BlockSpec(memory_space=pl.ANY)
@@ -488,28 +487,27 @@
     dma = pltpu.SemaphoreType.DMA
     width = LAT + 64
     scratch = [
-        V((NS, NH, width), BF), V((NSLOT, 512, width), BF), V((NH, LAT, VD), BF), V((NH * VD, 448), BF),
-        V((NBUF, SUF, width), BF),
+        V((NS, NH, width), BF), V((NH, LAT, VD), BF), V((448, NH * VD), BF),
+        V((NBUF, width, SUF), BF),
         V((NH, SP, NS * NH), BF), V((NH, SP, width), BF), V((PRE, SP, width), BF),
-        V((PRE, NSLOT, 16, 128), BF), V((PRE, NSLOT, 16, 128), BF),
         V((PRE * NSLOT, 16, 128), BF), V((PRE * NSLOT, 16, 128), BF),
         V((2, NPROMPT * 4, 16, 128), BF), V((2, NPROMPT, 16, 128), BF),
         V((PRE * NS, width), BF), V((NH, WIN, width), BF),
-        V((2, 8, PRE, 16, LAT), BF), V((8, PRE, 16, 128), BF),
+        V((8, width, 512), BF), V((1, PRE * SP), jnp.int32), V((PRE * NS, 1), jnp.int32),
         V((NS * NH, LAT), BF), V((NH, SP, LAT), BF), V((NH, SP, VD), BF), V((NH, 8, 128), F32),
         V((PRE, SP, VD), BF), V((PRE, 8, 128), F32), V((NH, 128), F32),
         V((NH, WIN, LAT), BF), V((NH, WIN, VD), BF), V((NH, 8, 128), F32),
         V((8, WIN, 2 * VD), BF), V((PRE, 8, 128), F32), V((NH, 128), F32),
         V((PRE * NS, VD), F32), V((PRE * NS, 128), F32), V((PRE * NS, NH * VD), BF),
         V((HEAD, WIN, 448), BF), V((HEAD, WIN, 448), BF),
-        dma((4,)), dma((NBUF,)), dma((10, PRE)), dma((10, PRE)),
+        dma((5,)), dma((NBUF,)), dma((10, PRE)), dma((10, PRE)),
         dma((2, 3)), dma((2, 3)), dma((2, 4)), dma((2, 4)),
         dma((2, 3)), dma((2, 3)), dma((2, 12)), dma((2, 12)), dma((HEAD,)), dma((HEAD,)),
     ]
     return pl.pallas_call(
         kernel,
         out_shape=jax.ShapeDtypeStruct((WIN, 448), BF),
-        in_specs=[hbm, hbm, hbm, hbm, hbm, vmem, vmem, smem, smem],
+        in_specs=[hbm, hbm, hbm, hbm, hbm, vmem, smem, smem],
         out_specs=vmem,
         scratch_shapes=scratch,
         compiler_params=pltpu.CompilerParams(
@@ -517,8 +515,8 @@
         ),
         cost_estimate=pl.CostEstimate(flops=10_000_000_000, bytes_accessed=30_000_000, transcendentals=3_000_000),
     )(
-        query_latent, prefix_cache, suffix_cache, value_map, out_weight,
-        rank_row, rank_col, block_slot.reshape(-1), suffix_length,
+        query_latent, prefix_cache.transpose(0, 2, 1), suffix_cache.transpose(0, 2, 1), value_map, out_weight.T,
+        prompt_row, block_slot.T, suffix_length,
     )
 
 

time: 183 us -> 143 us (0.78)
  local copies, waits for them, and re-layouts: 36.2 us -> 2.95 us
  Pallas kernels: 144 us -> 139 us
    unnamed x7 -> x1, local copies, waits for them, and re-layouts: 33.9 us -> 1.53 us
    pallas_call x1, Pallas kernels: 144 us -> 139 us  [per_device(): pl.pallas_call(kernel, out_shape=jax.ShapeDtypeStruct((WIN, 448), BF), in...]
where the time goes in v2:
time: 143 us; the launch traced here: 142 us
  Pallas kernels  139 us (97%)
  local copies, waits for them, and re-layouts  2.95 us (2%)
    pallas_call x1, Pallas kernels, per_device(): pl.pallas_call(kernel, out_shape=jax.ShapeDtypeStruct((WIN, 448), BF), in...  139 us

profile of v2, /device:TPU:1, one launch (start us, length us, event | category | flops | bytes accessed | tf_op | source)
XLA Modules:
  0.0 142.2 jit_solution(12538573798878960729)
XLA Ops:
  0.0 0.8 reshape.6
  0.8 0.7 reshape.7.prompt_row
  1.4 139.2 %shard_map.82 = bf16[80,448]{1,0:T(8,128)(2,1)} custom-call(bf16[40,16,576]{2,1,0:T(8,128)(2,1)} %q_hbm.1, bf16[5,576,512]{2,1,0:T(8,128)(2,1)} %bitcast.5, bf16[40,576,384]{2,1,0:T(8,128)(2,1)} %bitcast.4, bf16[16,512,128]{2,1,0:T(8,128)(2,1)} %vm_hbm.1, bf16[448,2048]{1,0:T(8,128)(2,1)} %bitcast.6, s32[1,768]{1,0:T(1,128)} %reshape.7.prompt_row, ...), custom_call_target="tpu_custom_call" | custom-call | flops 10000000000 | bytes 30000000 | tf_op jit(solution)/shard_map/pallas_call | solution.py:507
  140.6 1.5 %copy.10 = bf16[80,448]{1,0:T(8,128)(2,1)} copy(bf16[80,448]{1,0:T(8,128)(2,1)} %shard_map.82) | data formatting | bytes 143360
  (1 shorter events, 0.0 us)

commit v3 on v2

v3 whole, which is shorter than its diff:
```python
import functools
import math

import jax
import jax.numpy as jnp
from jax import lax
from jax.experimental import pallas as pl
from jax.experimental.pallas import tpu as pltpu
from jax.sharding import PartitionSpec as P

GROUP = 64
PRE = 16
HEAD = 8
NS = 40
SP = 48
NH = 16
LAT = 512
VD = 128
SUF = 384
WIN = 80
NSLOT = 5
NPROMPT = 10
NBUF = 4
MASKED = -1e30
GROUPS = ((0, 16, 0), (16, 32, 128), (48, 32, 384))
SCALE2 = math.log2(math.e) / math.sqrt(192.0)

BF = jnp.bfloat16
F32 = jnp.float32
MESH = pl.DeviceIdType.MESH


def nt(a, b):
    return lax.dot_general(a, b, (((1,), (1,)), ((), ())), preferred_element_type=F32)


def nn(a, b):
    return lax.dot_general(a, b, (((1,), (0,)), ((), ())), preferred_element_type=F32)


def onehot(mask):
    return jnp.where(mask, 1.0, 0.0).astype(BF)


def iota(shape, dim):
    return lax.broadcasted_iota(jnp.int32, shape, dim)


def kernel(
    q_hbm, k_hbm, suf_hbm, vm_hbm, w_hbm, prompt_row, slots, lens,
    out,
    q_in, vm, w_in, sufbuf,
    tmat, q_t, qr, krl, krr,
    skl, skr, sq, qw, kw, rank_row, rank_col, sort, unsort,
    lat_s, lt_s, o_s, l_s, osr, lsr, lacc_s,
    ol, op, lps, orr, lr, lacc,
    suf_rhs, suf, hbuf, part_o, pb, rs,
    ld_sem, suf_sem, a2a_s, a2a_r, x_s, x_r, c_s, c_r, g1_s, g1_r, g2_s, g2_r, e_s, e_r,
):
    p = lax.axis_index("pre")
    h = lax.axis_index("head")
    x, c = h // 2, lax.rem(h, 2)
    y, z = p // 4, lax.rem(p, 4)
    win, half = p // 2, lax.rem(p, 2)
    wj = lax.rem(win, 4)

    def remote(src, dst, ssem, rsem, pre, head):
        return pltpu.make_async_remote_copy(
            src_ref=src, dst_ref=dst, send_sem=ssem, recv_sem=rsem,
            device_id={"pre": pre, "head": head}, device_id_type=MESH,
        )

    def around(fn):
        def body(d, carry):
            fn(lax.rem(p + d, PRE))
            return carry
        lax.fori_loop(1, PRE, body, 0)

    def lane(i):
        return pl.ds(pl.multiple_of(i * 128, 128), 128)

    load_q = pltpu.make_async_copy(q_hbm, q_in, ld_sem.at[4])
    load_v = pltpu.make_async_copy(vm_hbm, vm, ld_sem.at[2])
    load_w = pltpu.make_async_copy(w_hbm, w_in, ld_sem.at[3])
    load_q.start()

    def suf_load(n, slot):
        return pltpu.make_async_copy(suf_hbm.at[n], sufbuf.at[slot], suf_sem.at[slot])

    barrier = pltpu.get_barrier_semaphore()

    def greet_pre(other):
        pl.semaphore_signal(barrier, inc=1, device_id={"pre": other, "head": h}, device_id_type=MESH)

    around(greet_pre)

    def greet_head(d, carry):
        pl.semaphore_signal(
            barrier, inc=1, device_id={"pre": p, "head": lax.rem(h + d, HEAD)}, device_id_type=MESH
        )
        return carry

    lax.fori_loop(1, HEAD, greet_head, 0)

    def build_t(i, carry):
        row = iota((SP, NS * NH), 0)
        col = iota((SP, NS * NH), 1)
        tmat[i] = onehot((lax.shift_right_logical(col, 4) == row) & ((col & 15) == i))
        return carry

    lax.fori_loop(0, NH, build_t, 0)

    lacc_s[...] = jnp.zeros_like(lacc_s)
    lacc[...] = jnp.zeros_like(lacc)

    load_q.wait()
    q_flat = q_in[...].reshape(NS * NH, LAT + 64)
    for g in range(2):
        t_part = tmat[g * 8:(g + 1) * 8].reshape(8 * SP, NS * NH)
        q_t[g * 8:(g + 1) * 8] = nn(t_part, q_flat).astype(BF).reshape(8, SP, LAT + 64)
    pl.semaphore_wait(barrier, PRE - 1 + HEAD - 1)

    def tiles(i):
        return (
            k_hbm.at[:, pl.ds(pl.multiple_of(c * 256 + i * 16, 16), 16), lane(x)],
            k_hbm.at[:, pl.ds(pl.multiple_of(LAT + lax.rem(i, 4) * 16, 16), 16), lane(x)],
        )

    def s1l(other, src):
        return remote(tiles(other)[0], krl.at[pl.ds(src * NSLOT, NSLOT)],
                      a2a_s.at[0, other], a2a_r.at[0, src], other, h)

    def s1r(other, src):
        return remote(tiles(other)[1], krr.at[pl.ds(src * NSLOT, NSLOT)],
                      a2a_s.at[1, other], a2a_r.at[1, src], other, h)

    def on_core0(fn):
        pl.when(c == 0)(lambda: around(fn))

    around(lambda other: s1l(other, p).start())
    on_core0(lambda other: s1r(other, p).start())
    own_l = pltpu.make_async_copy(tiles(p)[0], krl.at[pl.ds(p * NSLOT, NSLOT)], ld_sem.at[0])
    own_r = pltpu.make_async_copy(tiles(p)[1], krr.at[pl.ds(p * NSLOT, NSLOT)], ld_sem.at[1])
    own_l.start()
    own_r.start()

    names = jnp.broadcast_to(prompt_row[...], (SP, PRE * SP))
    at = iota((SP, PRE * SP), 1)
    rank_row[...] = prompt_row[...] * GROUP

    def build_rank(i, carry):
        ids = iota((SP, PRE * SP), 0) + i * SP
        name = jnp.sum(jnp.where(at == ids, names, 0), axis=1, keepdims=True)
        same = names == name
        before = jnp.sum(jnp.where(same & (at < ids), 1, 0), axis=1, keepdims=True)
        rank_col[pl.ds(pl.multiple_of(i * NS, 8), NS)] = (name * GROUP + before)[:NS]
        rank_row[...] += jnp.sum(jnp.where(same & (ids < at), 1, 0), axis=0, keepdims=True)
        return carry

    lax.fori_loop(0, PRE, build_rank, 0)
    def rank_of(place):
        r0 = 80 * lax.shift_right_logical(place, 4) + (place & 15)
        r1 = 80 * lax.shift_right_logical(place - 128, 5) + (place & 31) + 16
        r2 = 80 * lax.shift_right_logical(place - 384, 5) + (place & 31) + 48
        return jnp.where(place < 128, r0, jnp.where(place < 384, r1, r2))

    def build_sort(i, carry):
        rows = pl.ds(pl.multiple_of(i * 64, 64), 64)
        place = iota((64, 1), 0) + i * 64
        sort[rows] = onehot(rank_of(place) == rank_row[...])
        unsort[rows] = onehot(rank_col[rows] == rank_of(iota((1, PRE * NS), 1)))
        return carry

    lax.fori_loop(0, PRE * NS // 64, build_sort, 0)

    load_v.start()
    load_w.start()
    for n in range(NBUF):
        suf_load(n, n).start()

    def suffix_one(n, carry):
        slot = lax.rem(n, NBUF)
        suf_load(n, slot).wait()
        qn = q_in[n]
        kn = sufbuf[slot]
        t = nn(qn, kn) * SCALE2
        t = jnp.where(iota((NH, SUF), 1) < lens[n], t, MASKED)
        m = jnp.max(t, axis=1, keepdims=True)
        w = jnp.exp2(t - m).astype(BF)
        total = jnp.sum(w.astype(F32), axis=1, keepdims=True)
        o = nt(w, kn[:LAT]) / total
        lat_s[pl.ds(pl.multiple_of(n * NH, NH), NH)] = o.astype(BF)
        lse = m + jnp.log2(total)
        lacc_s[...] = jnp.where(iota((NH, 128), 1) == n, lse, lacc_s[...])

        @pl.when(n + NBUF < NS)
        def _():
            suf_load(n + NBUF, slot).start()

        return carry


    around(lambda other: s1l(other, other).wait_recv())
    on_core0(lambda other: s1r(other, other).wait_recv())
    own_l.wait()
    own_r.wait()

    def pick(prompt, carry):
        for b in range(8):
            slot = slots[b, prompt]
            skl[b // 4, prompt * 4 + b % 4] = krl[slot]
        for hf in range(2):
            skr[hf, prompt] = krr[slots[hf * 4 + p // 4, prompt]]
        return carry

    lax.fori_loop(0, NPROMPT, pick, 0)

    def first_of(other):
        return 5 * (other // 8) + lax.rem(other // 2, 4)

    def s2l(ab, other, src):
        rows = pl.ds(pl.multiple_of(c * 256 + src * 16, 16), 16)
        return remote(skl.at[lax.rem(other, 2), pl.ds((first_of(other) + ab) * 4, 4)],
                      kw.at[pl.ds(ab * 4, 4), rows, lane(x)],
                      a2a_s.at[3 + ab, other], a2a_r.at[3 + ab, src], other, h)

    def s2r(other, src):
        rows = pl.ds(pl.multiple_of(LAT + lax.rem(src, 4) * 16, 16), 16)
        return remote(skr.at[lax.rem(other, 2), pl.ds(first_of(other), 2)],
                      kw.reshape(2, 4, LAT + 64, 512).at[:, src // 4, rows, lane(x)],
                      a2a_s.at[5, other], a2a_r.at[5, src], other, h)

    own = first_of(p)
    for ab in range(2):
        around(lambda other: s2l(ab, other, p).start())
        if ab == 0:
            on_core0(lambda other: s2r(other, p).start())
    kw[:, pl.ds(pl.multiple_of(c * 256 + p * 16, 16), 16), lane(x)] = skl[half, pl.ds(own * 4, 8)]

    @pl.when(c == 0)
    def _():
        rows = pl.ds(pl.multiple_of(LAT + lax.rem(p, 4) * 16, 16), 16)
        kw[p // 4, rows, lane(x)] = skr[half, own]
        kw[p // 4 + 4, rows, lane(x)] = skr[half, own + 1]

    def s1q(other, src):
        return remote(q_t.at[other], qr.at[src], a2a_s.at[2, other], a2a_r.at[2, src], other, h)

    around(lambda other: s1q(other, p).start())
    qr[p] = q_t[p]

    lax.fori_loop(0, 6, suffix_one, 0)

    def views(cc, src_x):
        rows = pl.ds(pl.multiple_of(cc * 256, 256), 256)
        return kw.at[0:4, rows, lane(src_x)], kw.at[4:8, rows, lane(src_x)], kw.at[:, LAT:, lane(src_x)]

    def back(d):
        return lax.rem(x + 4 - d, 4)

    def x_copy(k, d, src_x):
        step = d if d != 2 or k == 2 else (1, 3)[k]
        view = views(c, src_x)[k]
        return remote(view, view, x_s.at[k, d - 1], x_r.at[k, d - 1], p, lax.rem(x + step, 4) * 2 + c)

    def core_copy(k, d, src_x, cc):
        view = views(cc, src_x)[k]
        return remote(view, view, c_s.at[k, d], c_r.at[k, d], p, x * 2 + (1 - c))

    def send_x(k):
        for d in (1, 3) if k < 2 else (1, 3, 2):
            x_copy(k, d, x).start()
        core_copy(k, 0, x, c).start()

    def pass_on(k, d):
        x_copy(k, d, back(d)).wait_recv()
        if (k, d) in ((0, 1), (1, 3)):
            x_copy(k, 2, back(d)).start()
        core_copy(k, d, back(d), c).start()

    def wait_core(k):
        for d in (0, 1, 3, 2):
            core_copy(k, d, back(d), 1 - c).wait_recv()

    def core0(fn):
        pl.when(c == 0)(fn)

    around(lambda other: s2l(0, other, other).wait_recv())
    send_x(0)
    around(lambda other: s2l(1, other, other).wait_recv())
    send_x(1)
    on_core0(lambda other: s2r(other, other).wait_recv())
    core0(lambda: send_x(2))
    lax.fori_loop(6, 12, suffix_one, 0)
    pass_on(0, 1)
    pass_on(0, 3)
    lax.fori_loop(12, 14, suffix_one, 0)

    around(lambda other: s1q(other, other).wait_recv())
    q_all = qr[...].reshape(PRE * SP, LAT + 64)

    def s2q(g, other, src):
        r0, nr, base = GROUPS[g]
        return remote(sq.at[pl.ds(pl.multiple_of(base + (other // 2) * nr, 16), nr)], qw.at[src, pl.ds(r0, nr)],
                      a2a_s.at[6 + g, other], a2a_r.at[6 + g, src], other, h)

    for g, (r0, nr, base) in enumerate(GROUPS):
        sq[base:base + 8 * nr] = nn(sort[base:base + 8 * nr], q_all).astype(BF)
        around(lambda other: s2q(g, other, p).start())
        qw[p, r0:r0 + nr] = sq[pl.ds(pl.multiple_of(base + win * nr, 16), nr)]

    pass_on(1, 3)
    pass_on(1, 1)
    lax.fori_loop(14, 24, suffix_one, 0)
    pass_on(0, 2)
    lax.fori_loop(24, 32, suffix_one, 0)
    pass_on(1, 2)

    @core0
    def _():
        for d in (1, 3, 2):
            pass_on(2, d)

    lax.fori_loop(32, NS, suffix_one, 0)

    load_v.wait()
    for g in range(2):
        t_part = tmat[g * 8:(g + 1) * 8].reshape(8 * SP, NS * NH)
        lt_s[g * 8:(g + 1) * 8] = nn(t_part, lat_s[...]).astype(BF).reshape(8, SP, LAT)

    def project_s(i, carry):
        o_s[i] = nn(lt_s[i], vm[i]).astype(BF)
        return carry

    lax.fori_loop(0, NH, project_s, 0)
    l_s[...] = lacc_s[...][:, None, :]

    def s4o(other, src):
        return remote(o_s.at[other], osr.at[src], a2a_s.at[9, other], a2a_r.at[9, src], other, h)

    def s4l(other, src):
        return remote(l_s.at[other], lsr.at[src], a2a_s.at[10, other], a2a_r.at[10, src], other, h)

    def start4(other):
        s4o(other, p).start()
        s4l(other, p).start()

    around(start4)
    osr[p] = o_s[p]
    lsr[p] = l_s[p]

    def spread(src, carry):
        rows = pl.ds(pl.multiple_of(src * SP, 16), SP)
        suf_rhs[rows, :VD] = osr[src]
        row = jnp.broadcast_to(lsr[src], (SP, 128))
        at = iota((SP, 128), 1)
        lse = jnp.sum(jnp.where(iota((SP, 128), 0) == at, row, 0.0), axis=1, keepdims=True)
        high = lse.astype(BF).astype(F32)
        middle = (lse - high).astype(BF).astype(F32)
        low = lse - high - middle
        terms = jnp.where(at == 0, high, jnp.where(at == 1, middle, jnp.where(at == 2, low, 0.0)))
        suf_rhs[rows, VD:] = terms.astype(BF)
        return carry

    def sort_suffix():
        def wait4(other):
            s4o(other, other).wait_recv()
            s4l(other, other).wait_recv()

        around(wait4)
        lax.fori_loop(0, PRE, spread, 0)
        suf[...] = nn(sort[...], suf_rhs[...])

    def chunk(g, t, carry):
        rows = pl.ds(pl.multiple_of(t * 16, 16), 16)
        ab = (t + wj) // 4
        qc = qw[:, rows].reshape(256, LAT + 64)
        scores = [nn(qc, kw[ab * 4 + b]) * SCALE2 for b in range(4)]
        m = functools.reduce(jnp.maximum, [jnp.max(t, axis=1, keepdims=True) for t in scores])
        total = jnp.zeros((256, 1), F32)
        acc = jnp.zeros((256, LAT), F32)
        for b in range(4):
            w = jnp.exp2(scores[b] - m).astype(BF)
            total = total + jnp.sum(w.astype(F32), axis=1, keepdims=True)
            acc = acc + nt(w, kw[ab * 4 + b, :LAT])
        ol[:, rows] = (acc / total).astype(BF).reshape(NH, 16, LAT)
        lse = (m + jnp.log2(total)).reshape(NH, 16, 1)
        here = iota((NH, 16, 128), 2) == iota((NH, 16, 128), 1) + (t * 16 - GROUPS[g][0])
        lacc[g] += jnp.sum(jnp.where(here, lse, 0.0), axis=1)
        return carry

    def s5o(g, other, src):
        r0, nr, base = GROUPS[g]
        rows = pl.ds(pl.multiple_of(base + (src // 2) * nr, 16), nr)
        return remote(op.at[other, pl.ds(r0, nr)], orr.at[rows, lane(lax.rem(src, 2))],
                      a2a_s.at[11 + g, other], a2a_r.at[11 + g, src], other, h)

    def s5l(g, other, src):
        return remote(lps.at[g, other], lr.at[g, lax.rem(src, 2), src // 2],
                      a2a_s.at[14 + g, other], a2a_r.at[14 + g, src], other, h)

    def attend(g):
        r0, nr, base = GROUPS[g]
        around(lambda other: s2q(g, other, other).wait_recv())
        lax.fori_loop(r0 // 16, (r0 + nr) // 16, functools.partial(chunk, g), 0)
        lps[g] = lacc[g][:, None, :]

        def start5(other):
            op[other, r0:r0 + nr] = nn(ol[other, r0:r0 + nr], vm[other]).astype(BF)
            s5o(g, other, p).start()
            s5l(g, other, p).start()

        around(start5)
        orr[pl.ds(pl.multiple_of(base + win * nr, 16), nr), lane(half)] = nn(ol[p, r0:r0 + nr], vm[p]).astype(BF)
        lr[g, half, win] = lps[g, p]

    def merge(g):
        r0, nr, base = GROUPS[g]

        def wait5(other):
            s5o(g, other, other).wait_recv()
            s5l(g, other, other).wait_recv()

        around(wait5)
        rows = slice(base, base + 8 * nr)
        eye = iota((8, nr, 128), 2) == iota((8, nr, 128), 1)

        def column(hf):
            spread_l = jnp.where(eye, jnp.broadcast_to(lr[g, hf], (8, nr, 128)), 0.0)
            return jnp.sum(spread_l, axis=2, keepdims=True).reshape(8 * nr, 1)

        la, lb = column(0), column(1)
        ls = jnp.sum(suf[rows, VD:], axis=1, keepdims=True)
        top = jnp.maximum(jnp.maximum(la, lb), ls)
        ea, eb, es = jnp.exp2(la - top), jnp.exp2(lb - top), jnp.exp2(ls - top)
        inv = 1.0 / (ea + eb + es)
        merged = (
            (ea * inv) * orr[rows, :VD].astype(F32)
            + (eb * inv) * orr[rows, VD:].astype(F32)
            + (es * inv) * suf[rows, :VD]
        )
        hbuf[rows, lane(p)] = merged.astype(BF)

    def g_copy(g, part, piece, dy, dz, ssem, rsem):
        _, nr, base = GROUPS[g]
        view = hbuf.at[pl.ds(base + part * 4 * nr, 4 * nr), lane(piece)]
        return remote(view, view, ssem, rsem, lax.rem(y + dy, 4) * 4 + lax.rem(z + dz, 4), h)

    def piece_of(by, bz):
        return lax.rem(y + 4 - by, 4) * 4 + lax.rem(z + 4 - bz, 4)

    def first(g, part, d, piece):
        dy, dz = (0, d) if part == 0 else (d, 0)
        return g_copy(g, part, piece, dy, dz, g1_s.at[g, part, d - 1], g1_r.at[g, part, d - 1])

    def second(g, part, k, d, piece):
        dy, dz = (d, 0) if part == 0 else (0, d)
        return g_copy(g, part, piece, dy, dz, g2_s.at[g, part, k * 3 + d - 1], g2_r.at[g, part, k * 3 + d - 1])

    def gather1(g):
        for d in (1, 3, 2):
            for part in range(2):
                first(g, part, d, p).start()
        for d in (1, 3, 2):
            for part in range(2):
                second(g, part, 0, d, p).start()

    def gather2(g):
        for k in (1, 3, 2):
            for part in range(2):
                got = piece_of(0, k) if part == 0 else piece_of(k, 0)
                first(g, part, k, got).wait_recv()
                for d in (1, 3, 2):
                    second(g, part, k, d, got).start()

    def gathered(g):
        for k in (0, 1, 3, 2):
            for d in (1, 3, 2):
                for part in range(2):
                    got = piece_of(d, k) if part == 0 else piece_of(k, d)
                    second(g, part, k, d, got).wait_recv()

    def out_rows(g):
        _, nr, base = GROUPS[g]
        rows = slice(base, base + 8 * nr)
        part_o[rows] = nt(hbuf[rows], w_in[...]).astype(BF)

    wait_core(0)
    wait_core(1)
    pl.when(c == 1)(lambda: wait_core(2))
    attend(0)
    sort_suffix()
    attend(1)
    merge(0)
    gather1(0)
    attend(2)
    gather2(0)
    merge(1)
    gather1(1)
    load_w.wait()
    gathered(0)
    out_rows(0)
    merge(2)
    gather1(2)
    gather2(1)
    gather2(2)
    gathered(1)
    out_rows(1)
    gathered(2)
    out_rows(2)

    for g in range(2):
        pb[g * 4:(g + 1) * 4] = nn(unsort[g * 320:(g + 1) * 320], part_o[...]).astype(BF).reshape(4, WIN, 448)

    def s6(other, src):
        return remote(pb.at[other], rs.at[src], e_s.at[other], e_r.at[src], p, other)

    def heads(fn):
        def body(d, carry):
            fn(lax.rem(h + d, HEAD))
            return carry
        lax.fori_loop(1, HEAD, body, 0)

    heads(lambda other: s6(other, h).start())
    rs[h] = pb[h]
    heads(lambda other: s6(other, other).wait_recv())
    total = rs[0].astype(F32)
    for k in range(1, HEAD):
        total = total + rs[k].astype(F32)
    out[...] = total.astype(BF)

    def sent(other):
        for copy in (s1l, s1q, s4o, s4l):
            copy(other, p).wait_send()
        for ab in range(2):
            s2l(ab, other, p).wait_send()
        for g in range(3):
            for copy in (s2q, s5o, s5l):
                copy(g, other, p).wait_send()

    around(sent)
    on_core0(lambda other: s1r(other, p).wait_send())
    on_core0(lambda other: s2r(other, p).wait_send())

    def sent_blocks(k):
        for d in (1, 2, 3):
            x_copy(k, d, x).wait_send()
        for d in range(4):
            core_copy(k, d, back(d), c).wait_send()

    sent_blocks(0)
    sent_blocks(1)
    core0(lambda: sent_blocks(2))
    for g in range(3):
        for part in range(2):
            for d in (1, 2, 3):
                first(g, part, d, p).wait_send()
            for k in range(4):
                for d in (1, 2, 3):
                    second(g, part, k, d, p).wait_send()
    heads(lambda other: s6(other, h).wait_send())


def per_device(
    query_latent, prefix_cache, block_slot, sample_prompt, suffix_cache, suffix_length, value_map, out_weight
):
    prompt_row = jnp.pad(
        sample_prompt.reshape(PRE, NS), ((0, 0), (0, SP - NS)), constant_values=-4
    ).reshape(1, PRE * SP)
    vmem = pl.BlockSpec(memory_space=pltpu.VMEM)
    smem = pl.BlockSpec(memory_space=pltpu.SMEM)
    hbm = pl.BlockSpec(memory_space=pl.ANY)
    V = pltpu.VMEM
    dma = pltpu.SemaphoreType.DMA
    width = LAT + 64
    scratch = [
        V((NS, NH, width), BF), V((NH, LAT, VD), BF), V((448, NH * VD), BF),
        V((NBUF, width, SUF), BF),
        V((NH, SP, NS * NH), BF), V((NH, SP, width), BF), V((PRE, SP, width), BF),
        V((PRE * NSLOT, 16, 128), BF), V((PRE * NSLOT, 16, 128), BF),
        V((2, NPROMPT * 4, 16, 128), BF), V((2, NPROMPT, 16, 128), BF),
        V((PRE * NS, width), BF), V((NH, WIN, width), BF),
        V((8, width, 512), BF), V((1, PRE * SP), jnp.int32), V((PRE * NS, 1), jnp.int32),
        V((PRE * NS, PRE * SP), BF), V((PRE * NS, PRE * NS), BF),
        V((NS * NH, LAT), BF), V((NH, SP, LAT), BF), V((NH, SP, VD), BF), V((NH, 1, 128), F32),
        V((PRE, SP, VD), BF), V((PRE, 1, 128), F32), V((NH, 128), F32),
        V((NH, WIN, LAT), BF), V((NH, WIN, VD), BF), V((3, NH, 1, 128), F32),
        V((PRE * NS, 2 * VD), BF), V((3, 2, 8, 1, 128), F32), V((3, NH, 128), F32),
        V((PRE * SP, 2 * VD), BF), V((PRE * NS, 2 * VD), F32), V((PRE * NS, NH * VD), BF),
        V((PRE * NS, 448), BF), V((HEAD, WIN, 448), BF), V((HEAD, WIN, 448), BF),
        dma((5,)), dma((NBUF,)), dma((17, PRE)), dma((17, PRE)),
        dma((3, 3)), dma((3, 3)), dma((3, 4)), dma((3, 4)),
        dma((3, 2, 3)), dma((3, 2, 3)), dma((3, 2, 12)), dma((3, 2, 12)), dma((HEAD,)), dma((HEAD,)),
    ]
    return pl.pallas_call(
        kernel,
        out_shape=jax.ShapeDtypeStruct((WIN, 448), BF),
        in_specs=[hbm, hbm, hbm, hbm, hbm, vmem, smem, smem],
        out_specs=vmem,
        scratch_shapes=scratch,
        compiler_params=pltpu.CompilerParams(
            collective_id=0, has_side_effects=True, vmem_limit_bytes=58 * 1024 * 1024
        ),
        cost_estimate=pl.CostEstimate(flops=10_000_000_000, bytes_accessed=30_000_000, transcendentals=3_000_000),
    )(
        query_latent, prefix_cache.transpose(0, 2, 1), suffix_cache.transpose(0, 2, 1), value_map, out_weight.T,
        prompt_row, block_slot.T, suffix_length,
    )


def solution(mesh):
    return jax.shard_map(
        per_device,
        mesh=mesh,
        in_specs=(
            P("pre", "head", None),
            P("pre", None, None),
            P(),
            P(),
            P("pre", None, None),
            P("pre"),
            P("head", None, None),
            P("head", "pre"),
        ),
        out_specs=P("head", "pre"),
        check_vma=False,
    )
```

time: 143 us -> 115 us (0.80)
  Pallas kernels: 139 us -> 112 us
    pallas_call x1, Pallas kernels: 139 us -> 112 us  [per_device(): pl.pallas_call(kernel, out_shape=jax.ShapeDtypeStruct((WIN, 448), BF), in...]
where the time goes in v3:
time: 115 us
  Pallas kernels  112 us (97%)
  local copies, waits for them, and re-layouts  2.95 us (3%)
    pallas_call x1, Pallas kernels, per_device(): pl.pallas_call(kernel, out_shape=jax.ShapeDtypeStruct((WIN, 448), BF), in...  112 us

profile of v3, /device:TPU:1, one launch (start us, length us, event | category | flops | bytes accessed | tf_op | source)
XLA Modules:
  0.0 115.1 jit_solution(14117872030072174677)
XLA Ops:
  0.0 0.8 reshape.6
  0.8 0.7 reshape.7.prompt_row
  1.4 112.1 %shard_map.82 = bf16[80,448]{1,0:T(8,128)(2,1)} custom-call(bf16[40,16,576]{2,1,0:T(8,128)(2,1)} %q_hbm.1, bf16[5,576,512]{2,1,0:T(8,128)(2,1)} %bitcast.5, bf16[40,576,384]{2,1,0:T(8,128)(2,1)} %bitcast.4, bf16[16,512,128]{2,1,0:T(8,128)(2,1)} %vm_hbm.1, bf16[448,2048]{1,0:T(8,128)(2,1)} %bitcast.6, s32[1,768]{1,0:T(1,128)} %reshape.7.prompt_row, ...), custom_call_target="tpu_custom_call" | custom-call | flops 10000000000 | bytes 30000000 | tf_op jit(solution)/shard_map/pallas_call | solution.py:595
  113.6 1.5 %copy.10 = bf16[80,448]{1,0:T(8,128)(2,1)} copy(bf16[80,448]{1,0:T(8,128)(2,1)} %shard_map.82) | data formatting | bytes 143360
  (1 shorter events, 0.0 us)

commit v4 on v3

--- a/solution.py
+++ b/solution.py
@@ -54,7 +54,7 @@
     skl, skr, sq, qw, kw, rank_row, rank_col, sort, unsort,
     lat_s, lt_s, o_s, l_s, osr, lsr, lacc_s,
     ol, op, lps, orr, lr, lacc,
-    suf_rhs, suf, hbuf, part_o, pb, rs,
+    suf_rhs, suf, hbuf, part_o, pb, cb, xb, rs,
     ld_sem, suf_sem, a2a_s, a2a_r, x_s, x_r, c_s, c_r, g1_s, g1_r, g2_s, g2_r, e_s, e_r,
 ):
     p = lax.axis_index("pre")
@@ -102,22 +102,9 @@
 
     lax.fori_loop(1, HEAD, greet_head, 0)
 
-    def build_t(i, carry):
-        row = iota((SP, NS * NH), 0)
-        col = iota((SP, NS * NH), 1)
-        tmat[i] = onehot((lax.shift_right_logical(col, 4) == row) & ((col & 15) == i))
-        return carry
-
-    lax.fori_loop(0, NH, build_t, 0)
-
     lacc_s[...] = jnp.zeros_like(lacc_s)
     lacc[...] = jnp.zeros_like(lacc)
 
-    load_q.wait()
-    q_flat = q_in[...].reshape(NS * NH, LAT + 64)
-    for g in range(2):
-        t_part = tmat[g * 8:(g + 1) * 8].reshape(8 * SP, NS * NH)
-        q_t[g * 8:(g + 1) * 8] = nn(t_part, q_flat).astype(BF).reshape(8, SP, LAT + 64)
     pl.semaphore_wait(barrier, PRE - 1 + HEAD - 1)
 
     def tiles(i):
@@ -144,6 +131,19 @@
     own_l.start()
     own_r.start()
 
+    def build_t(i, carry):
+        row = iota((SP, NS * NH), 0)
+        col = iota((SP, NS * NH), 1)
+        tmat[i] = onehot((lax.shift_right_logical(col, 4) == row) & ((col & 15) == i))
+        return carry
+
+    lax.fori_loop(0, NH, build_t, 0)
+
+    load_q.wait()
+    q_flat = q_in[...].reshape(NS * NH, LAT + 64)
+    for g in range(2):
+        t_part = tmat[g * 8:(g + 1) * 8].reshape(8 * SP, NS * NH)
+        q_t[g * 8:(g + 1) * 8] = nn(t_part, q_flat).astype(BF).reshape(8, SP, LAT + 64)
     names = jnp.broadcast_to(prompt_row[...], (SP, PRE * SP))
     at = iota((SP, PRE * SP), 1)
     rank_row[...] = prompt_row[...] * GROUP
@@ -178,27 +178,33 @@
     for n in range(NBUF):
         suf_load(n, n).start()
 
-    def suffix_one(n, carry):
-        slot = lax.rem(n, NBUF)
-        suf_load(n, slot).wait()
-        qn = q_in[n]
-        kn = sufbuf[slot]
-        t = nn(qn, kn) * SCALE2
-        t = jnp.where(iota((NH, SUF), 1) < lens[n], t, MASKED)
-        m = jnp.max(t, axis=1, keepdims=True)
-        w = jnp.exp2(t - m).astype(BF)
-        total = jnp.sum(w.astype(F32), axis=1, keepdims=True)
-        o = nt(w, kn[:LAT]) / total
-        lat_s[pl.ds(pl.multiple_of(n * NH, NH), NH)] = o.astype(BF)
-        lse = m + jnp.log2(total)
-        lacc_s[...] = jnp.where(iota((NH, 128), 1) == n, lse, lacc_s[...])
-
-        @pl.when(n + NBUF < NS)
+    def suffix_pair(pair, carry):
+        ns = (2 * pair, 2 * pair + 1)
+        slots_of = [lax.rem(n, NBUF) for n in ns]
+        for n, slot in zip(ns, slots_of):
+            suf_load(n, slot).wait()
+        keys = [sufbuf[slot] for slot in slots_of]
+        ts = [nn(q_in[n], kn) * SCALE2 for n, kn in zip(ns, keys)]
+        ts = [jnp.where(iota((NH, SUF), 1) < lens[n], t, MASKED) for n, t in zip(ns, ts)]
+        ms = [jnp.max(t, axis=1, keepdims=True) for t in ts]
+        ws = [jnp.exp2(t - m).astype(BF) for t, m in zip(ts, ms)]
+        totals = [jnp.sum(w.astype(F32), axis=1, keepdims=True) for w in ws]
+        outs = [nt(w, kn[:LAT]) for w, kn in zip(ws, keys)]
+        both = jnp.concatenate([o / total for o, total in zip(outs, totals)], axis=0)
+        lat_s[pl.ds(pl.multiple_of(pair * 2 * NH, 2 * NH), 2 * NH)] = both.astype(BF)
+        at = iota((NH, 128), 1)
+        lse = [m + jnp.log2(total) for m, total in zip(ms, totals)]
+        lacc_s[...] = jnp.where(at == ns[0], lse[0], jnp.where(at == ns[1], lse[1], lacc_s[...]))
+
+        @pl.when(ns[0] + NBUF < NS)
         def _():
-            suf_load(n + NBUF, slot).start()
-
-        return carry
-
+            for n, slot in zip(ns, slots_of):
+                suf_load(n + NBUF, slot).start()
+
+        return carry
+
+    def suffix(first, last):
+        lax.fori_loop(first // 2, last // 2, suffix_pair, 0)
 
     around(lambda other: s1l(other, other).wait_recv())
     on_core0(lambda other: s1r(other, other).wait_recv())
@@ -249,7 +255,7 @@
     around(lambda other: s1q(other, p).start())
     qr[p] = q_t[p]
 
-    lax.fori_loop(0, 6, suffix_one, 0)
+    suffix(0, 6)
 
     def views(cc, src_x):
         rows = pl.ds(pl.multiple_of(cc * 256, 256), 256)
@@ -287,14 +293,14 @@
 
     around(lambda other: s2l(0, other, other).wait_recv())
     send_x(0)
+    on_core0(lambda other: s2r(other, other).wait_recv())
+    core0(lambda: send_x(2))
     around(lambda other: s2l(1, other, other).wait_recv())
     send_x(1)
-    on_core0(lambda other: s2r(other, other).wait_recv())
-    core0(lambda: send_x(2))
-    lax.fori_loop(6, 12, suffix_one, 0)
+    suffix(6, 12)
     pass_on(0, 1)
     pass_on(0, 3)
-    lax.fori_loop(12, 14, suffix_one, 0)
+    suffix(12, 18)
 
     around(lambda other: s1q(other, other).wait_recv())
     q_all = qr[...].reshape(PRE * SP, LAT + 64)
@@ -306,34 +312,28 @@
 
     for g, (r0, nr, base) in enumerate(GROUPS):
         sq[base:base + 8 * nr] = nn(sort[base:base + 8 * nr], q_all).astype(BF)
-        around(lambda other: s2q(g, other, p).start())
+        if g == 0:
+            around(lambda other: s2q(g, other, p).start())
         qw[p, r0:r0 + nr] = sq[pl.ds(pl.multiple_of(base + win * nr, 16), nr)]
-
-    pass_on(1, 3)
-    pass_on(1, 1)
-    lax.fori_loop(14, 24, suffix_one, 0)
-    pass_on(0, 2)
-    lax.fori_loop(24, 32, suffix_one, 0)
-    pass_on(1, 2)
 
     @core0
     def _():
         for d in (1, 3, 2):
             pass_on(2, d)
 
-    lax.fori_loop(32, NS, suffix_one, 0)
-
-    load_v.wait()
-    for g in range(2):
-        t_part = tmat[g * 8:(g + 1) * 8].reshape(8 * SP, NS * NH)
-        lt_s[g * 8:(g + 1) * 8] = nn(t_part, lat_s[...]).astype(BF).reshape(8, SP, LAT)
-
-    def project_s(i, carry):
-        o_s[i] = nn(lt_s[i], vm[i]).astype(BF)
-        return carry
-
-    lax.fori_loop(0, NH, project_s, 0)
-    l_s[...] = lacc_s[...][:, None, :]
+    def next_group(g):
+        around(lambda other: s2q(g - 1, other, p).wait_send())
+        around(lambda other: s2q(g, other, p).start())
+
+    pass_on(1, 3)
+    suffix(18, 22)
+    next_group(1)
+    suffix(22, 26)
+    pass_on(0, 2)
+    pass_on(1, 1)
+    suffix(26, 34)
+    next_group(2)
+    suffix(34, NS)
 
     def s4o(other, src):
         return remote(o_s.at[other], osr.at[src], a2a_s.at[9, other], a2a_r.at[9, src], other, h)
@@ -344,10 +344,6 @@
     def start4(other):
         s4o(other, p).start()
         s4l(other, p).start()
-
-    around(start4)
-    osr[p] = o_s[p]
-    lsr[p] = l_s[p]
 
     def spread(src, carry):
         rows = pl.ds(pl.multiple_of(src * SP, 16), SP)
@@ -405,13 +401,15 @@
         lax.fori_loop(r0 // 16, (r0 + nr) // 16, functools.partial(chunk, g), 0)
         lps[g] = lacc[g][:, None, :]
 
+        for i in range(NH):
+            op[i, r0:r0 + nr] = nn(ol[i, r0:r0 + nr], vm[i]).astype(BF)
+
         def start5(other):
-            op[other, r0:r0 + nr] = nn(ol[other, r0:r0 + nr], vm[other]).astype(BF)
             s5o(g, other, p).start()
             s5l(g, other, p).start()
 
         around(start5)
-        orr[pl.ds(pl.multiple_of(base + win * nr, 16), nr), lane(half)] = nn(ol[p, r0:r0 + nr], vm[p]).astype(BF)
+        orr[pl.ds(pl.multiple_of(base + win * nr, 16), nr), lane(half)] = op[p, r0:r0 + nr]
         lr[g, half, win] = lps[g, p]
 
     def merge(g):
@@ -439,70 +437,82 @@
             + (eb * inv) * orr[rows, VD:].astype(F32)
             + (es * inv) * suf[rows, :VD]
         )
-        hbuf[rows, lane(p)] = merged.astype(BF)
-
-    def g_copy(g, part, piece, dy, dz, ssem, rsem):
+        hbuf[y, z, rows] = merged.astype(BF)
+
+    def half_rows(g, part):
         _, nr, base = GROUPS[g]
-        view = hbuf.at[pl.ds(base + part * 4 * nr, 4 * nr), lane(piece)]
-        return remote(view, view, ssem, rsem, lax.rem(y + dy, 4) * 4 + lax.rem(z + dz, 4), h)
-
-    def piece_of(by, bz):
-        return lax.rem(y + 4 - by, 4) * 4 + lax.rem(z + 4 - bz, 4)
-
-    def first(g, part, d, piece):
+        return pl.ds(base + part * 4 * nr, 4 * nr)
+
+    def first(g, part, d, src_y, src_z):
         dy, dz = (0, d) if part == 0 else (d, 0)
-        return g_copy(g, part, piece, dy, dz, g1_s.at[g, part, d - 1], g1_r.at[g, part, d - 1])
-
-    def second(g, part, k, d, piece):
+        view = hbuf.at[src_y, src_z, half_rows(g, part)]
+        return remote(view, view, g1_s.at[g, part, d - 1], g1_r.at[g, part, d - 1],
+                      lax.rem(y + dy, 4) * 4 + lax.rem(z + dz, 4), h)
+
+    def second(g, part, d, src):
+        rows = half_rows(g, part)
         dy, dz = (d, 0) if part == 0 else (0, d)
-        return g_copy(g, part, piece, dy, dz, g2_s.at[g, part, k * 3 + d - 1], g2_r.at[g, part, k * 3 + d - 1])
+        view = hbuf.at[src, :, rows] if part == 0 else hbuf.at[:, src, rows]
+        return remote(view, view, g2_s.at[g, part, d - 1], g2_r.at[g, part, d - 1],
+                      lax.rem(y + dy, 4) * 4 + lax.rem(z + dz, 4), h)
 
     def gather1(g):
+        for d in (2, 1, 3):
+            for part in range(2):
+                first(g, part, d, y, z).start()
+
+    def gather2(g):
+        for part in range(2):
+            for d in (1, 3, 2):
+                at_z = lax.rem(z + 4 - d, 4) if part == 0 else z
+                at_y = lax.rem(y + 4 - d, 4) if part == 1 else y
+                first(g, part, d, at_y, at_z).wait_recv()
+            for d in (2, 1, 3):
+                second(g, part, d, (y, z)[part]).start()
+
+    def gathered(g):
         for d in (1, 3, 2):
             for part in range(2):
-                first(g, part, d, p).start()
-        for d in (1, 3, 2):
-            for part in range(2):
-                second(g, part, 0, d, p).start()
-
-    def gather2(g):
-        for k in (1, 3, 2):
-            for part in range(2):
-                got = piece_of(0, k) if part == 0 else piece_of(k, 0)
-                first(g, part, k, got).wait_recv()
-                for d in (1, 3, 2):
-                    second(g, part, k, d, got).start()
-
-    def gathered(g):
-        for k in (0, 1, 3, 2):
-            for d in (1, 3, 2):
-                for part in range(2):
-                    got = piece_of(d, k) if part == 0 else piece_of(k, d)
-                    second(g, part, k, d, got).wait_recv()
+                second(g, part, d, lax.rem((y, z)[part] + 4 - d, 4)).wait_recv()
 
     def out_rows(g):
         _, nr, base = GROUPS[g]
         rows = slice(base, base + 8 * nr)
-        part_o[rows] = nt(hbuf[rows], w_in[...]).astype(BF)
-
+        merged = jnp.concatenate([hbuf[k // 4, k % 4, rows] for k in range(PRE)], axis=1)
+        part_o[rows] = nt(merged, w_in[...]).astype(BF)
+
+    pass_on(1, 2)
     wait_core(0)
+    pl.when(c == 1)(lambda: wait_core(2))
+    load_v.wait()
+    attend(0)
+    for g in range(2):
+        t_part = tmat[g * 8:(g + 1) * 8].reshape(8 * SP, NS * NH)
+        lt_s[g * 8:(g + 1) * 8] = nn(t_part, lat_s[...]).astype(BF).reshape(8, SP, LAT)
+
+    for i in range(NH):
+        o_s[i] = nn(lt_s[i], vm[i]).astype(BF)
+    l_s[...] = lacc_s[...][:, None, :]
+
+    around(start4)
+    osr[p] = o_s[p]
+    lsr[p] = l_s[p]
+
     wait_core(1)
-    pl.when(c == 1)(lambda: wait_core(2))
-    attend(0)
+    attend(1)
     sort_suffix()
-    attend(1)
     merge(0)
     gather1(0)
     attend(2)
     gather2(0)
     merge(1)
     gather1(1)
+    merge(2)
+    gather1(2)
+    gather2(1)
     load_w.wait()
     gathered(0)
     out_rows(0)
-    merge(2)
-    gather1(2)
-    gather2(1)
     gather2(2)
     gathered(1)
     out_rows(1)
@@ -510,33 +520,30 @@
     out_rows(2)
 
     for g in range(2):
-        pb[g * 4:(g + 1) * 4] = nn(unsort[g * 320:(g + 1) * 320], part_o[...]).astype(BF).reshape(4, WIN, 448)
-
-    def s6(other, src):
-        return remote(pb.at[other], rs.at[src], e_s.at[other], e_r.at[src], p, other)
-
-    def heads(fn):
-        def body(d, carry):
-            fn(lax.rem(h + d, HEAD))
-            return carry
-        lax.fori_loop(1, HEAD, body, 0)
-
-    heads(lambda other: s6(other, h).start())
-    rs[h] = pb[h]
-    heads(lambda other: s6(other, other).wait_recv())
-    total = rs[0].astype(F32)
-    for k in range(1, HEAD):
-        total = total + rs[k].astype(F32)
-    out[...] = total.astype(BF)
-
+        rows = nn(unsort[g * 320:(g + 1) * 320], part_o[...]).astype(BF)
+        for k in range(4):
+            pb[k % 2, g * 2 + k // 2] = rows[k * WIN:(k + 1) * WIN]
+    swap = remote(pb.at[1 - c], cb, e_s.at[0], e_r.at[0], p, x * 2 + (1 - c))
+    swap.start()
+    swap.wait_recv()
+
+    def s6(d, src_x):
+        to = lax.rem(x + d, 4)
+        return remote(xb.at[to], rs.at[src_x], e_s.at[d], e_r.at[d], p, to * 2 + c)
+
+    for d in (2, 1, 3):
+        to = lax.rem(x + d, 4)
+        xb[to] = (pb[c, to].astype(F32) + cb[to].astype(F32)).astype(BF)
+        s6(d, x).start()
     def sent(other):
         for copy in (s1l, s1q, s4o, s4l):
             copy(other, p).wait_send()
         for ab in range(2):
             s2l(ab, other, p).wait_send()
         for g in range(3):
-            for copy in (s2q, s5o, s5l):
+            for copy in (s5o, s5l):
                 copy(g, other, p).wait_send()
+        s2q(2, other, p).wait_send()
 
     around(sent)
     on_core0(lambda other: s1r(other, p).wait_send())
@@ -554,11 +561,18 @@
     for g in range(3):
         for part in range(2):
             for d in (1, 2, 3):
-                first(g, part, d, p).wait_send()
-            for k in range(4):
-                for d in (1, 2, 3):
-                    second(g, part, k, d, p).wait_send()
-    heads(lambda other: s6(other, h).wait_send())
+                first(g, part, d, y, z).wait_send()
+                second(g, part, d, (y, z)[part]).wait_send()
+
+    total = pb[c, x].astype(F32) + cb[x].astype(F32)
+    for d in (1, 3, 2):
+        s6(d, back(d)).wait_recv()
+        total = total + rs[back(d)].astype(F32)
+    out[...] = total.astype(BF)
+
+    swap.wait_send()
+    for d in (1, 2, 3):
+        s6(d, x).wait_send()
 
 
 def per_device(
@@ -586,11 +600,11 @@
         V((PRE, SP, VD), BF), V((PRE, 1, 128), F32), V((NH, 128), F32),
         V((NH, WIN, LAT), BF), V((NH, WIN, VD), BF), V((3, NH, 1, 128), F32),
         V((PRE * NS, 2 * VD), BF), V((3, 2, 8, 1, 128), F32), V((3, NH, 128), F32),
-        V((PRE * SP, 2 * VD), BF), V((PRE * NS, 2 * VD), F32), V((PRE * NS, NH * VD), BF),
-        V((PRE * NS, 448), BF), V((HEAD, WIN, 448), BF), V((HEAD, WIN, 448), BF),
+        V((PRE * SP, 2 * VD), BF), V((PRE * NS, 2 * VD), F32), V((4, 4, PRE * NS, VD), BF),
+        V((PRE * NS, 448), BF), V((2, 4, WIN, 448), BF), V((4, WIN, 448), BF), V((4, WIN, 448), BF), V((4, WIN, 448), BF),
         dma((5,)), dma((NBUF,)), dma((17, PRE)), dma((17, PRE)),
         dma((3, 3)), dma((3, 3)), dma((3, 4)), dma((3, 4)),
-        dma((3, 2, 3)), dma((3, 2, 3)), dma((3, 2, 12)), dma((3, 2, 12)), dma((HEAD,)), dma((HEAD,)),
+        dma((3, 2, 3)), dma((3, 2, 3)), dma((3, 2, 3)), dma((3, 2, 3)), dma((4,)), dma((4,)),
     ]
     return pl.pallas_call(
         kernel,

time: 115 us -> 107 us (0.930)
  Pallas kernels: 112 us -> 104 us
    pallas_call x1, Pallas kernels: 112 us -> 104 us  [per_device(): pl.pallas_call(kernel, out_shape=jax.ShapeDtypeStruct((WIN, 448), BF), in...]
where the time goes in v4:
time: 107 us
  Pallas kernels  104 us (97%)
  local copies, waits for them, and re-layouts  2.95 us (3%)
    pallas_call x1, Pallas kernels, per_device(): pl.pallas_call(kernel, out_shape=jax.ShapeDtypeStruct((WIN, 448), BF), in...  104 us

profile of v4, /device:TPU:1, one launch (start us, length us, event | category | flops | bytes accessed | tf_op | source)
XLA Modules:
  0.0 107.1 jit_solution(10580633620688380517)
XLA Ops:
  0.0 0.8 reshape.6
  0.8 0.7 reshape.7.prompt_row
  1.4 104.1 %shard_map.82 = bf16[80,448]{1,0:T(8,128)(2,1)} custom-call(bf16[40,16,576]{2,1,0:T(8,128)(2,1)} %q_hbm.1, bf16[5,576,512]{2,1,0:T(8,128)(2,1)} %bitcast.5, bf16[40,576,384]{2,1,0:T(8,128)(2,1)} %bitcast.4, bf16[16,512,128]{2,1,0:T(8,128)(2,1)} %vm_hbm.1, bf16[448,2048]{1,0:T(8,128)(2,1)} %bitcast.6, s32[1,768]{1,0:T(1,128)} %reshape.7.prompt_row, ...), custom_call_target="tpu_custom_call" | custom-call | flops 10000000000 | bytes 30000000 | tf_op jit(solution)/shard_map/pallas_call | solution.py:609
  105.6 1.5 %copy.10 = bf16[80,448]{1,0:T(8,128)(2,1)} copy(bf16[80,448]{1,0:T(8,128)(2,1)} %shard_map.82) | data formatting | bytes 143360
  (1 shorter events, 0.0 us)

commit v5 on v4

--- a/solution.py
+++ b/solution.py
@@ -47,7 +47,7 @@
 
 
 def kernel(
-    q_hbm, k_hbm, suf_hbm, vm_hbm, w_hbm, prompt_row, slots, lens,
+    q_hbm, k_hbm, suf_hbm, vm_hbm, w_hbm, prompts, slots, lens,
     out,
     q_in, vm, w_in, sufbuf,
     tmat, q_t, qr, krl, krr,
@@ -144,9 +144,14 @@
     for g in range(2):
         t_part = tmat[g * 8:(g + 1) * 8].reshape(8 * SP, NS * NH)
         q_t[g * 8:(g + 1) * 8] = nn(t_part, q_flat).astype(BF).reshape(8, SP, LAT + 64)
-    names = jnp.broadcast_to(prompt_row[...], (SP, PRE * SP))
+    pieces = [jnp.full((1, 128), -4, jnp.int32) for _ in range(PRE * SP // 128)]
+    for n in range(PRE * NS):
+        tile, at = divmod(n // NS * SP + n % NS, 128)
+        pieces[tile] = jnp.where(iota((1, 128), 1) == at, prompts[n], pieces[tile])
+    prompt_row = jnp.concatenate(pieces, axis=1)
+    names = jnp.broadcast_to(prompt_row, (SP, PRE * SP))
     at = iota((SP, PRE * SP), 1)
-    rank_row[...] = prompt_row[...] * GROUP
+    rank_row[...] = prompt_row * GROUP
 
     def build_rank(i, carry):
         ids = iota((SP, PRE * SP), 0) + i * SP
@@ -578,9 +583,6 @@
 def per_device(
     query_latent, prefix_cache, block_slot, sample_prompt, suffix_cache, suffix_length, value_map, out_weight
 ):
-    prompt_row = jnp.pad(
-        sample_prompt.reshape(PRE, NS), ((0, 0), (0, SP - NS)), constant_values=-4
-    ).reshape(1, PRE * SP)
     vmem = pl.BlockSpec(memory_space=pltpu.VMEM)
     smem = pl.BlockSpec(memory_space=pltpu.SMEM)
     hbm = pl.BlockSpec(memory_space=pl.ANY)
@@ -609,7 +611,7 @@
     return pl.pallas_call(
         kernel,
         out_shape=jax.ShapeDtypeStruct((WIN, 448), BF),
-        in_specs=[hbm, hbm, hbm, hbm, hbm, vmem, smem, smem],
+        in_specs=[hbm, hbm, hbm, hbm, hbm, smem, smem, smem],
         out_specs=vmem,
         scratch_shapes=scratch,
         compiler_params=pltpu.CompilerParams(
@@ -618,7 +620,7 @@
         cost_estimate=pl.CostEstimate(flops=10_000_000_000, bytes_accessed=30_000_000, transcendentals=3_000_000),
     )(
         query_latent, prefix_cache.transpose(0, 2, 1), suffix_cache.transpose(0, 2, 1), value_map, out_weight.T,
-        prompt_row, block_slot.T, suffix_length,
+        sample_prompt, block_slot.T, suffix_length,
     )
 
 

time: 107 us -> 106 us (level)
  local copies, waits for them, and re-layouts: 2.95 us -> 1.53 us
    reshape x2 -> x0, local copies, waits for them, and re-layouts: 1.42 us -> none  [the longest x1 0.76 us: per_device(): sample_prompt.reshape(PRE, NS)]
where the time goes in v5:
time: 106 us
  Pallas kernels  104 us (98%)
  local copies, waits for them, and re-layouts  1.53 us (1%)
    pallas_call x1, Pallas kernels, per_device(): pl.pallas_call(kernel, out_shape=jax.ShapeDtypeStruct((WIN, 448), BF), in...  104 us

profile of v5, /device:TPU:1, one launch (start us, length us, event | category | flops | bytes accessed | tf_op | source)
XLA Modules:
  0.0 105.9 jit_solution(1817644866280988821)
XLA Ops:
  0.0 104.3 %shard_map.82 = bf16[80,448]{1,0:T(8,128)(2,1)} custom-call(bf16[40,16,576]{2,1,0:T(8,128)(2,1)} %q_hbm.1, bf16[5,576,512]{2,1,0:T(8,128)(2,1)} %bitcast.5, bf16[40,576,384]{2,1,0:T(8,128)(2,1)} %bitcast.4, bf16[16,512,128]{2,1,0:T(8,128)(2,1)} %vm_hbm.1, bf16[448,2048]{1,0:T(8,128)(2,1)} %bitcast.6, s32[640]{0:T(1024)} %prompts.1, s32[8,10]{1,0:T(8,128)} %bitcast.7, ...), custom_call_target="tpu_custom_call" | custom-call | flops 10000000000 | bytes 30000000 | tf_op jit(solution)/shard_map/pallas_call | solution.py:611
  104.3 1.5 %copy.10 = bf16[80,448]{1,0:T(8,128)(2,1)} copy(bf16[80,448]{1,0:T(8,128)(2,1)} %shard_map.82) | data formatting | bytes 143360

commit v6 on v5

--- a/solution.py
+++ b/solution.py
@@ -164,10 +164,12 @@
 
     lax.fori_loop(0, PRE, build_rank, 0)
     def rank_of(place):
-        r0 = 80 * lax.shift_right_logical(place, 4) + (place & 15)
-        r1 = 80 * lax.shift_right_logical(place - 128, 5) + (place & 31) + 16
-        r2 = 80 * lax.shift_right_logical(place - 384, 5) + (place & 31) + 48
-        return jnp.where(place < 128, r0, jnp.where(place < 384, r1, r2))
+        w = jnp.where(
+            place < 128, lax.shift_right_logical(place, 4),
+            jnp.where(place < 384, lax.shift_right_logical(place - 128, 5), lax.shift_right_logical(place - 384, 5)),
+        )
+        u = jnp.where(place < 128, place & 15, jnp.where(place < 384, (place & 31) + 16, (place & 31) + 48))
+        return 80 * w + jnp.where((w & 3) < 2, u, 64 - u + 2 * (u & 15))
 
     def build_sort(i, carry):
         rows = pl.ds(pl.multiple_of(i * 64, 64), 64)
@@ -221,7 +223,9 @@
             slot = slots[b, prompt]
             skl[b // 4, prompt * 4 + b % 4] = krl[slot]
         for hf in range(2):
-            skr[hf, prompt] = krr[slots[hf * 4 + p // 4, prompt]]
+            tile = krr[slots[hf * 4 + p // 4, prompt]]
+            skr[hf, 0, prompt] = tile
+            skr[hf, 1, NPROMPT - 1 - prompt] = tile
         return carry
 
     lax.fori_loop(0, NPROMPT, pick, 0)
@@ -229,15 +233,21 @@
     def first_of(other):
         return 5 * (other // 8) + lax.rem(other // 2, 4)
 
+    def backwards(other):
+        return lax.rem(other // 2, 4) // 2
+
+    def rope_from(other):
+        return first_of(other) + backwards(other) * (NPROMPT - 2 - 2 * first_of(other))
+
     def s2l(ab, other, src):
         rows = pl.ds(pl.multiple_of(c * 256 + src * 16, 16), 16)
-        return remote(skl.at[lax.rem(other, 2), pl.ds((first_of(other) + ab) * 4, 4)],
+        return remote(skl.at[lax.rem(other, 2), pl.ds((first_of(other) + lax.rem(ab + backwards(other), 2)) * 4, 4)],
                       kw.at[pl.ds(ab * 4, 4), rows, lane(x)],
                       a2a_s.at[3 + ab, other], a2a_r.at[3 + ab, src], other, h)
 
     def s2r(other, src):
         rows = pl.ds(pl.multiple_of(LAT + lax.rem(src, 4) * 16, 16), 16)
-        return remote(skr.at[lax.rem(other, 2), pl.ds(first_of(other), 2)],
+        return remote(skr.at[lax.rem(other, 2), backwards(other), pl.ds(rope_from(other), 2)],
                       kw.reshape(2, 4, LAT + 64, 512).at[:, src // 4, rows, lane(x)],
                       a2a_s.at[5, other], a2a_r.at[5, src], other, h)
 
@@ -246,13 +256,16 @@
         around(lambda other: s2l(ab, other, p).start())
         if ab == 0:
             on_core0(lambda other: s2r(other, p).start())
-    kw[:, pl.ds(pl.multiple_of(c * 256 + p * 16, 16), 16), lane(x)] = skl[half, pl.ds(own * 4, 8)]
+    for ab in range(2):
+        kw[ab * 4:ab * 4 + 4, pl.ds(pl.multiple_of(c * 256 + p * 16, 16), 16), lane(x)] = skl[
+            half, pl.ds((own + lax.rem(ab + backwards(p), 2)) * 4, 4)
+        ]
 
     @pl.when(c == 0)
     def _():
         rows = pl.ds(pl.multiple_of(LAT + lax.rem(p, 4) * 16, 16), 16)
-        kw[p // 4, rows, lane(x)] = skr[half, own]
-        kw[p // 4 + 4, rows, lane(x)] = skr[half, own + 1]
+        kw[p // 4, rows, lane(x)] = skr[half, backwards(p), rope_from(p)]
+        kw[p // 4 + 4, rows, lane(x)] = skr[half, backwards(p), rope_from(p) + 1]
 
     def s1q(other, src):
         return remote(q_t.at[other], qr.at[src], a2a_s.at[2, other], a2a_r.at[2, src], other, h)
@@ -374,7 +387,7 @@
 
     def chunk(g, t, carry):
         rows = pl.ds(pl.multiple_of(t * 16, 16), 16)
-        ab = (t + wj) // 4
+        ab = jnp.where(wj < 2, (t + wj) // 4, 1 - (4 - t + wj) // 4)
         qc = qw[:, rows].reshape(256, LAT + 64)
         scores = [nn(qc, kw[ab * 4 + b]) * SCALE2 for b in range(4)]
         m = functools.reduce(jnp.maximum, [jnp.max(t, axis=1, keepdims=True) for t in scores])
@@ -486,7 +499,6 @@
         merged = jnp.concatenate([hbuf[k // 4, k % 4, rows] for k in range(PRE)], axis=1)
         part_o[rows] = nt(merged, w_in[...]).astype(BF)
 
-    pass_on(1, 2)
     wait_core(0)
     pl.when(c == 1)(lambda: wait_core(2))
     load_v.wait()
@@ -503,11 +515,12 @@
     osr[p] = o_s[p]
     lsr[p] = l_s[p]
 
-    wait_core(1)
+    pass_on(1, 2)
     attend(1)
     sort_suffix()
     merge(0)
     gather1(0)
+    wait_core(1)
     attend(2)
     gather2(0)
     merge(1)
@@ -594,7 +607,7 @@
         V((NBUF, width, SUF), BF),
         V((NH, SP, NS * NH), BF), V((NH, SP, width), BF), V((PRE, SP, width), BF),
         V((PRE * NSLOT, 16, 128), BF), V((PRE * NSLOT, 16, 128), BF),
-        V((2, NPROMPT * 4, 16, 128), BF), V((2, NPROMPT, 16, 128), BF),
+        V((2, NPROMPT * 4, 16, 128), BF), V((2, 2, NPROMPT, 16, 128), BF),
         V((PRE * NS, width), BF), V((NH, WIN, width), BF),
         V((8, width, 512), BF), V((1, PRE * SP), jnp.int32), V((PRE * NS, 1), jnp.int32),
         V((PRE * NS, PRE * SP), BF), V((PRE * NS, PRE * NS), BF),

time: 106 us -> 106 us (level)
  no operation moved by 1% of the time
where the time goes in v6:
time: 106 us
  Pallas kernels  104 us (98%)
  local copies, waits for them, and re-layouts  1.53 us (1%)
    pallas_call x1, Pallas kernels, per_device(): pl.pallas_call(kernel, out_shape=jax.ShapeDtypeStruct((WIN, 448), BF), in...  104 us

profile of v6, /device:TPU:1, one launch (start us, length us, event | category | flops | bytes accessed | tf_op | source)
XLA Modules:
  0.0 105.6 jit_solution(7783392796719665323)
XLA Ops:
  0.0 104.1 %shard_map.82 = bf16[80,448]{1,0:T(8,128)(2,1)} custom-call(bf16[40,16,576]{2,1,0:T(8,128)(2,1)} %q_hbm.1, bf16[5,576,512]{2,1,0:T(8,128)(2,1)} %bitcast.5, bf16[40,576,384]{2,1,0:T(8,128)(2,1)} %bitcast.4, bf16[16,512,128]{2,1,0:T(8,128)(2,1)} %vm_hbm.1, bf16[448,2048]{1,0:T(8,128)(2,1)} %bitcast.6, s32[640]{0:T(1024)} %prompts.1, s32[8,10]{1,0:T(8,128)} %bitcast.7, ...), custom_call_target="tpu_custom_call" | custom-call | flops 10000000000 | bytes 30000000 | tf_op jit(solution)/shard_map/pallas_call | solution.py:624
  104.1 1.5 %copy.10 = bf16[80,448]{1,0:T(8,128)(2,1)} copy(bf16[80,448]{1,0:T(8,128)(2,1)} %shard_map.82) | data formatting | bytes 143360
